TPU v7x, 32 devices: a whole 2x2x4 slice. The times are simulated.
32 devices in a mesh: seq: 16 (over z, y, x), ffn: 2 (over core).
Axes of the slice: x: 2, y: 2, z: 4, core: 2. Of those that a mesh axis runs over, the one named last changes fastest.
Arguments:
- patches: bfloat16 [4096, 4096], P('seq'), may hold values from -100 to 100
- gate_weight: bfloat16 [4096, 7168], P('seq', 'ffn'), may hold values from -0.09375 to 0.09375
- up_weight: bfloat16 [4096, 7168], P('seq', 'ffn'), may hold values from -0.09375 to 0.09375
- down_weight: bfloat16 [4096, 7168], P('seq', 'ffn'), may hold values from -0.25 to 0.25
- key_weight: bfloat16 [4096, 1024], P(None, 'ffn'), may hold values from -0.09375 to 0.09375
- value_weight: bfloat16 [4096, 1024], P(None, 'ffn'), may hold values from -0.09375 to 0.09375
- byte_states: bfloat16 [32768, 1024], P('seq'), may hold values from -60 to 60
- byte_patch: int32 [32768], P('seq'), may hold values from 0 to 4095, as said below
- cross_query: bfloat16 [1024, 1024], P(None, 'ffn'), may hold values from -0.375 to 0.375
- self_query: bfloat16 [1024, 1024], P(None, 'ffn'), may hold values from -0.375 to 0.375
- self_key: bfloat16 [1024, 1024], P(None, 'ffn'), may hold values from -0.375 to 0.375
- self_value: bfloat16 [1024, 1024], P(None, 'ffn'), may hold values from -0.1875 to 0.1875
- cross_out: bfloat16 [1024, 1024], P('ffn'), may hold values from -0.1875 to 0.1875
- self_out: bfloat16 [1024, 1024], P('ffn'), may hold values from -0.1875 to 0.1875
Outputs:
- update: bfloat16 [32768, 1024], P('seq', 'ffn')
Inputs may be any that keep to these rules, and one draw needn't show every extreme that they name: byte_patch starts at 0, never falls, rises by at most 1 from one byte to the next and ends at 4095, so every patch is a run of one or more bytes. The bytes s * 2048 to (s + 1) * 2048 - 1 read only patches s * 256 - 23 to (s + 1) * 256 + 15; both ends are reached in every draw.
All inputs are finite; a program needn't handle non-finite values.
Results may differ from a plain program's by a relative error of at most 0.0085.
The roundings to bfloat16 on the way count: a program that leaves them out, or rounds other values in their place, can miss the bound.
Values may be sent and summed in bfloat16 or wider, within the bound.
A program may use at most 192 MiB of HBM per device.

v0:
```python
import math

import jax
import jax.numpy as jnp
from jax import lax
from jax.sharding import PartitionSpec as P

HD = 64
PWIN = 8
WINDOW = 512
HALO = 23


EPS = 1e-05


def padded(value, sides, width):
    for axis, dim in sides:
        count, length = (lax.axis_size(axis), value.shape[dim])
        up = [(i, (i + 1) % count) for i in range(count - 1)]
        down = [(j, i) for i, j in up]
        last = lax.slice_in_dim(value, length - width, length, axis=dim)
        first = lax.slice_in_dim(value, 0, width, axis=dim)
        before = lax.ppermute(last, axis, up)
        after = lax.ppermute(first, axis, down)
        value = jnp.concatenate([before, value, after], axis=dim)
    return value


def shifted(value, axis, by):
    count = lax.axis_size(axis)
    pairs = [(i, i + by) for i in range(count) if 0 <= i + by < count]
    return lax.ppermute(value, axis, pairs)


def row_normalize(matrix):
    widened = matrix.astype(jnp.float32)
    return widened * lax.rsqrt(jnp.mean(widened * widened, axis=-1, keepdims=True) + EPS)


def masked_softmax(scores, key_mask):
    masked = jnp.where(key_mask, scores, -jnp.inf)
    row_max = jnp.max(masked, axis=-1, keepdims=True)
    exp_terms = jnp.exp(masked - row_max)
    return exp_terms / jnp.sum(exp_terms, axis=-1, keepdims=True)


def local(
    patches,
    gate_weight,
    up_weight,
    down_weight,
    key_weight,
    value_weight,
    byte_states,
    byte_patch,
    cross_query,
    self_query,
    self_key,
    self_value,
    cross_out,
    self_out,
):
    patch_count = patches.shape[0]
    normed = row_normalize(patches).astype(jnp.bfloat16)

    def add_rows(piece_rows):
        return jnp.dot(normed, piece_rows, preferred_element_type=jnp.float32)

    gate_sum = add_rows(lax.all_gather(gate_weight, "seq", axis=0, tiled=True))
    up_sum = add_rows(lax.all_gather(up_weight, "seq", axis=0, tiled=True))
    hidden = (jax.nn.silu(gate_sum) * up_sum).astype(jnp.bfloat16)
    ffn_out = lax.dot_general(
        hidden,
        lax.all_gather(down_weight, "seq", axis=0, tiled=True),
        (((1,), (1,)), ((), ())),
        preferred_element_type=jnp.float32,
    )
    ffn_whole = lax.psum(ffn_out, "ffn")
    global_out = (patches.astype(jnp.float32) + ffn_whole).astype(jnp.bfloat16)
    head_cols = key_weight.shape[1]
    head_count = head_cols // HD
    score_scale = 1.0 / math.sqrt(HD)
    seq_index = lax.axis_index("seq")
    keys_c = jnp.dot(global_out, key_weight, preferred_element_type=jnp.float32).astype(
        jnp.bfloat16
    )
    values_c = jnp.dot(global_out, value_weight, preferred_element_type=jnp.float32).astype(
        jnp.bfloat16
    )
    both_c = jnp.concatenate([keys_c, values_c], axis=1)
    extended = padded(both_c, (("seq", 0),), HALO)
    key_count = extended.shape[0]
    key_index = seq_index * patch_count - HALO + jnp.arange(key_count, dtype=jnp.int32)
    cross_mask = (
        (key_index[None, :] <= byte_patch[:, None])
        & (key_index[None, :] > byte_patch[:, None] - PWIN)
        & (key_index[None, :] >= 0)
    )
    byte_count = byte_states.shape[0]
    query_c = jnp.dot(byte_states, cross_query, preferred_element_type=jnp.float32).astype(
        jnp.bfloat16
    )
    query_s = jnp.dot(byte_states, self_query, preferred_element_type=jnp.float32).astype(
        jnp.bfloat16
    )
    keys_s = jnp.dot(byte_states, self_key, preferred_element_type=jnp.float32).astype(jnp.bfloat16)
    values_s = jnp.dot(byte_states, self_value, preferred_element_type=jnp.float32).astype(
        jnp.bfloat16
    )
    query_here = query_c.reshape(byte_count, head_count, HD)
    keys_here = extended[:, :head_cols].reshape(key_count, head_count, HD)
    values_here = extended[:, head_cols:].reshape(key_count, head_count, HD)
    cross_scores = (
        jnp.einsum("qhd,khd->hqk", query_here, keys_here, preferred_element_type=jnp.float32)
        * score_scale
    )
    weights_c = masked_softmax(cross_scores, cross_mask[None]).astype(jnp.bfloat16)
    context_c = jnp.einsum(
        "hqk,khd->qhd", weights_c, values_here, preferred_element_type=jnp.float32
    )
    context_c = context_c.astype(jnp.bfloat16).reshape(byte_count, head_cols)
    both_s = jnp.concatenate([keys_s, values_s], axis=1)
    tail_rows = both_s[byte_count - WINDOW :]
    before = shifted(tail_rows, "seq", 1)
    stacked = jnp.concatenate([before, both_s], axis=0)
    blocks = byte_count // WINDOW
    lower_half = stacked[:byte_count].reshape(blocks, WINDOW, 2 * head_cols)
    upper_half = stacked[WINDOW:].reshape(blocks, WINDOW, 2 * head_cols)
    key_pairs = jnp.concatenate([lower_half, upper_half], axis=1)
    window_keys = key_pairs[:, :, :head_cols].reshape(blocks, 2 * WINDOW, head_count, HD)
    window_values = key_pairs[:, :, head_cols:].reshape(blocks, 2 * WINDOW, head_count, HD)
    window_queries = query_s.reshape(blocks, WINDOW, head_count, HD)
    self_scores = (
        jnp.einsum(
            "bqhd,bkhd->bhqk", window_queries, window_keys, preferred_element_type=jnp.float32
        )
        * score_scale
    )
    query_slot = jnp.arange(WINDOW, dtype=jnp.int32)[:, None]
    key_slot = jnp.arange(2 * WINDOW, dtype=jnp.int32)[None, :]
    band_mask = (key_slot > query_slot) & (key_slot <= query_slot + WINDOW)
    block_ids = jnp.arange(blocks, dtype=jnp.int32)
    key_pos = (
        seq_index * byte_count
        - WINDOW
        + block_ids[:, None] * WINDOW
        + jnp.arange(2 * WINDOW, dtype=jnp.int32)[None, :]
    )
    self_mask = band_mask[None, None] & (key_pos >= 0)[:, None, None, :]
    weights_s = masked_softmax(self_scores, self_mask).astype(jnp.bfloat16)
    context_s = jnp.einsum(
        "bhqk,bkhd->bqhd", weights_s, window_values, preferred_element_type=jnp.float32
    )
    context_s = context_s.astype(jnp.bfloat16).reshape(byte_count, head_cols)
    partial_sum = jnp.dot(context_c, cross_out, preferred_element_type=jnp.float32) + jnp.dot(
        context_s, self_out, preferred_element_type=jnp.float32
    )
    return lax.psum_scatter(partial_sum, "ffn", scatter_dimension=1, tiled=True).astype(
        jnp.bfloat16
    )


def solution(mesh):
    placed = (
        P("seq", None),
        P("seq", "ffn"),
        P("seq", "ffn"),
        P("seq", "ffn"),
        P(None, "ffn"),
        P(None, "ffn"),
        P("seq", None),
        P("seq"),
        P(None, "ffn"),
        P(None, "ffn"),
        P(None, "ffn"),
        P(None, "ffn"),
        P("ffn", None),
        P("ffn", None),
    )
    return jax.shard_map(
        local, mesh=mesh, in_specs=placed, out_specs=P("seq", "ffn"), check_vma=False
    )
```

profile of v0, /device:TPU:23, one launch (start us, length us, event | category | flops | bytes accessed | tf_op | source)
XLA Modules:
  0.0 1132.2 jit_solution(16112676747630708834)
XLA Ops:
  6.5 0.0 all-gather.4.cloned.1.call-start
  6.5 0.7 all-gather.4.cloned.1.call-update
  7.3 0.0 all-gather.6.cloned.1.call-start
  7.3 0.7 all-gather.6.cloned.1.call-update
  8.0 0.0 all-gather.8.cloned.1.call-start
  8.1 0.7 all-gather.8.cloned.1.call-update
  8.8 0.0 all-reduce.2.cloned.1.call-start
  8.8 0.0 copy-start.14
  8.8 4.7 convolution_convert_fusion.1
  13.6 2.5 convolution_convert_fusion.2
  16.1 0.0 copy-start.18
  16.1 1.1 fusion.33
  17.2 0.6 copy-done.6
  17.8 3.3 collective-permute-start.2
  21.1 6.2 convolution_convert_fusion
  27.3 6.4 reshape.197
  33.8 0.5 fusion.15
  34.3 0.1 add_compare_fusion
  34.3 0.0 copy-done.13
  34.4 0.4 fusion.31
  34.8 2.2 broadcast_and_fusion
  37.0 1.5 and_and_fusion
  38.5 3.8 convolution_convert_fusion.3
  42.3 39.8 %collective-permute-done.2 = bf16[512,1024]{0,1:T(8,128)(2,1)} collective-permute-done((bf16[512,1024]{0,1:T(8,128)(2,1)}, bf16[512,1024]{0,1:T(8,128)(2,1)}, u32[]{:S(2)}, u32[]{:S(2)}) %collective-permute-start.2) | collective-permute-done | bytes 1048608 | tf_op jit(solution)/shard_map/ppermute | solution.py:33
  82.1 21.4 %pad_maximum_fusion = (bf16[2048,1024]{0,1:T(8,128)(2,1)}, bf16[2048,1024]{0,1:T(8,128)(2,1)}) fusion(bf16[2048,512]{0,1:T(8,128)(2,1)S(1)} %copy-done.5, bf16[2048,512]{0,1:T(8,128)(2,1)S(1)} %copy-done.7, bf16[512,1024]{0,1:T(8,128)(2,1)} %collective-permute-done.2), kind=kLoop, calls=%fused_computation.25 | loop fusion | flops 20971520 | bytes 13631488 | tf_op jit(solution)/shard_map/concatenate | solution.py:123
  103.5 7.8 reshape.191
  111.3 8.3 reshape.192
  119.6 3.8 constant_dynamic-update-slice_fusion.1
  123.4 1.8 constant_dynamic-update-slice_fusion
  125.2 3.0 fusion.47
  128.2 3.4 copy.24
  131.5 3.4 copy.22
  134.9 205.0 %all-gather.4.cloned.1.call-done = bf16[4096,3584]{1,0:T(8,128)(2,1)} async-done(((bf16[256,3584]{1,0:T(8,128)(2,1)}), bf16[4096,3584]{1,0:T(8,128)(2,1)}) %all-gather.4.cloned.1.call-update) | async-done | bytes 29360144 | tf_op jit(solution)/shard_map/all_gather | solution.py:70
  339.9 15.1 %fusion.36 = f32[256,3584]{1,0:T(8,128)} fusion(bf16[4096,3584]{1,0:T(8,128)(2,1)} %all-gather.4.cloned.1.call-done, bf16[256,4096]{1,0:T(8,128)(2,1)S(1)} %copy-done.1, f32[256]{0:T(256)S(1)} %add_rsqrt_fusion), kind=kOutput, calls=%fused_computation.56 | convolution fusion | flops 7519338496 | bytes 35128320 | tf_op jit(solution)/shard_map/dot_general | solution.py:68
  355.1 297.0 %all-gather.6.cloned.1.call-done = bf16[4096,3584]{1,0:T(8,128)(2,1)} async-done(((bf16[256,3584]{1,0:T(8,128)(2,1)}), bf16[4096,3584]{1,0:T(8,128)(2,1)}) %all-gather.6.cloned.1.call-update) | async-done | bytes 29360144 | tf_op jit(solution)/shard_map/all_gather | solution.py:71
  652.0 312.1 %all-gather.8.cloned.1.call-done = bf16[4096,3584]{1,0:T(8,128)(2,1)} async-done(((bf16[256,3584]{1,0:T(8,128)(2,1)}), bf16[4096,3584]{1,0:T(8,128)(2,1)}) %all-gather.8.cloned.1.call-update) | async-done | bytes 29360144 | tf_op jit(solution)/shard_map/all_gather | solution.py:75
  964.2 30.5 %fusion.25 = f32[256,4096]{1,0:T(8,128)} fusion(bf16[4096,3584]{1,0:T(8,128)(2,1)} %all-gather.8.cloned.1.call-done, bf16[4096,3584]{1,0:T(8,128)(2,1)} %all-gather.6.cloned.1.call-done, f32[256,3584]{1,0:T(8,128)} %fusion.36, bf16[256,4096]{1,0:T(8,128)(2,1)S(1)} %copy-done.1, f32[256]{0:T(256)S(1)} %add_rsqrt_fusion), kind=kOutput, calls=%fused_computation.37 | convolution fusion | flops 15041036288 | bytes 68682752 | tf_op jit(solution)/shard_map/dot_general | solution.py:73
  994.7 0.0 all-reduce.2.cloned.1.call-update
  994.7 0.0 reduce-scatter.2.cloned.1.call-start
  994.7 32.3 %fusion.50 = (f32[4,8,512]{2,1,0:T(8,128)}, f32[4,8,512,1024]{3,2,1,0:T(8,128)}) fusion(pred[4,512,1024]{2,1,0:T(8,128)(4,1)} %broadcast_and_fusion, bf16[4,1024,8,64]{1,3,2,0:T(8,128)(2,1)} %bitcast.47, bf16[4,512,8,64]{3,2,1,0:T(8,128)(2,1)} %reshape.197), kind=kOutput, calls=%fused_computation.78 | convolution fusion | flops 2214593536 | bytes 75563008 | tf_op jit(solution)/shard_map/sub | solution.py:44
  1027.0 4.8 convolution_convert_fusion.4
  1031.9 1.1 copy-done.8
  1032.9 1.3 convolution_convert_fusion.5
  1034.3 0.7 copy-done.9
  1035.0 0.6 pad_maximum_fusion.5
  1035.6 3.1 collective-permute-start
  1038.8 2.1 collective-permute-start.1
  1040.9 24.7 %convert_bitcast_fusion = bf16[4,512,8,64]{1,3,2,0:T(8,128)(2,1)S(1)} fusion(bf16[4,1024,8,64]{1,3,2,0:T(8,128)(2,1)} %bitcast.46, f32[4,8,512,1024]{3,2,1,0:T(8,128)} %get-tuple-element.16, f32[4,8,512]{2,1,0:T(8,128)} %get-tuple-element.15), kind=kOutput, calls=%fused_computation.48 | convolution fusion | flops 2182086656 | bytes 73465856 | tf_op jit(solution)/shard_map/bhqk,bkhd->bqhd/dot_general | solution.py:152
  1065.6 1.6 copy.26
  1067.2 0.6 copy.29
  1067.8 0.0 collective-permute-done
  1067.8 0.0 collective-permute-done.1
  1067.9 0.1 pad_maximum_fusion.3
  1068.0 0.8 fusion.48
  1068.8 1.9 copy.21
  1070.7 0.9 copy.20
  1071.6 13.9 %fusion.49 = (f32[8,2048]{1,0:T(8,128)}, f32[8,2048,302]{1,2,0:T(8,128)}) fusion(pred[2048,302]{0,1:T(8,128)(4,1)} %and_and_fusion, bf16[2048,8,64]{0,2,1:T(8,128)(2,1)} %bitcast.50, bf16[302,8,64]{0,2,1:T(8,128)(2,1)} %bitcast.48), kind=kOutput, calls=%fused_computation.77 | convolution fusion | flops 653132096 | bytes 22882304 | tf_op jit(solution)/shard_map/sub | solution.py:44
  1085.5 8.8 fusion.30
  1094.3 0.0 copy-start.11
  1094.3 2.4 fusion.55
  1096.8 5.9 convolution_add_fusion
  1102.7 0.0 reduce-scatter.2.cloned.1.call-update
  1102.7 18.9 %reduce-scatter.2.cloned.1.call-done = f32[2048,512]{1,0:T(8,128)} async-done(((f32[2048,1024]{1,0:T(8,128)}), f32[2048,512]{1,0:T(8,128)}) %reduce-scatter.2.cloned.1.call-update) | async-done | bytes 4194320 | tf_op jit(solution)/shard_map/reduce_scatter | solution.py:159
  1121.6 3.8 convert_element_type.68
  (40 shorter events, 0.1 us)
Async XLA Ops:
  6.5 1087.8 %copy-start = (bf16[512,1024]{1,0:T(8,128)(2,1)S(1)}, bf16[512,1024]{1,0:T(8,128)(2,1)}, u32[]{:S(2)}) copy-start(bf16[512,1024]{1,0:T(8,128)(2,1)} %param.26) | copy-start | bytes 3145732
  6.5 2.3 copy-start.16
  6.5 333.4 %all-gather.4.cloned.1.call-start = ((), (), s32[]{:S(2)}) async-start(), calls=%async_computation.1 | async-start | bytes 31195136 | tf_op jit(solution)/shard_map/all_gather | solution.py:70
  7.3 644.8 %all-gather.6.cloned.1.call-start = ((), (), s32[]{:S(2)}) async-start(), calls=%async_computation.2 | async-start | bytes 31195136 | tf_op jit(solution)/shard_map/all_gather | solution.py:71
  8.0 956.1 %all-gather.8.cloned.1.call-start = ((), (), s32[]{:S(2)}) async-start(), calls=%async_computation.3 | async-start | bytes 31195136 | tf_op jit(solution)/shard_map/all_gather | solution.py:75
  8.7 4.8 copy-start.17
  8.8 1018.2 %all-reduce.2.cloned.1.call-start = ((), (), s32[]{:S(2)}) async-start(), calls=%async_computation.4 | async-start | bytes 8388608 | tf_op jit(solution)/shard_map/psum | solution.py:79
  8.8 4.8 copy-start.14
  13.6 2.5 copy-start.4
  16.1 1.7 copy-start.6
  16.1 5.0 copy-start.18
  17.8 64.3 %collective-permute-start.2 = (bf16[512,1024]{0,1:T(8,128)(2,1)}, bf16[512,1024]{0,1:T(8,128)(2,1)}, u32[]{:S(2)}, u32[]{:S(2)}) collective-permute-start(bf16[512,1024]{0,1:T(8,128)(2,1)} %fusion.33), channel_id=1, source_target_pairs={{0,2},{2,4},{4,6},{6,8},{8,10},{10,12},{12,14},{14,16},{16,18},{18... | collective-permute-start | bytes 3145736 | tf_op jit(solution)/shard_map/ppermute | solution.py:33
  27.3 6.4 copy-start.1
  27.3 7.0 copy-start.13
  33.7 4.8 copy-start.15
  33.7 4.8 copy-start.19
  38.5 43.6 %copy-start.5 = (bf16[2048,512]{0,1:T(8,128)(2,1)S(1)}, bf16[2048,512]{0,1:T(8,128)(2,1)}, u32[]{:S(2)}) copy-start(bf16[2048,512]{0,1:T(8,128)(2,1)} %copy-done.4) | copy-start | bytes 6291460
  38.5 43.6 %copy-start.7 = (bf16[2048,512]{0,1:T(8,128)(2,1)S(1)}, bf16[2048,512]{0,1:T(8,128)(2,1)}, u32[]{:S(2)}) copy-start(bf16[2048,512]{0,1:T(8,128)(2,1)} %copy-done.6) | copy-start | bytes 6291460
  119.6 3.8 copy-start.2
  994.7 127.0 %reduce-scatter.2.cloned.1.call-start = ((), (), s32[]{:S(2)}) async-start(), calls=%async_computation.5 | async-start | bytes 12582912 | tf_op jit(solution)/shard_map/reduce_scatter | solution.py:159
  1027.0 4.9 copy-start.3
  1027.0 5.9 copy-start.8
  1034.3 0.7 copy-start.9
  1035.6 32.2 %collective-permute-start = (bf16[23,1024]{1,0:T(8,128)(2,1)}, bf16[23,1024]{1,0:T(8,128)(2,1)S(1)}, u32[]{:S(2)}, u32[]{:S(2)}) collective-permute-start(bf16[23,1024]{1,0:T(8,128)(2,1)} %get-tuple-element.11), channel_id=1, source_target_pairs={{0,2},{2,4},{4,6},{6,8},{8,10},{10,12},{12,14},{14,16},{16,18},{18... | collective-permute-start | bytes 141320 | tf_op jit(solution)/shard_map/ppermute | solution.py:24
  1038.8 29.1 %collective-permute-start.1 = (bf16[23,1024]{1,0:T(8,128)(2,1)S(1)}, bf16[23,1024]{1,0:T(8,128)(2,1)S(1)}, u32[]{:S(2)}, u32[]{:S(2)}) collective-permute-start(bf16[23,1024]{1,0:T(8,128)(2,1)S(1)} %get-tuple-element.12), channel_id=1, source_target_pairs={{2,0},{4,2},{6,4},{8,6},{10,8},{12,10},{14,12},{16,14},{18,16},{20... | collective-permute-start | bytes 141320 | tf_op jit(solution)/shard_map/ppermute | solution.py:25
  1065.6 2.3 copy-start.10
  1071.6 13.9 %copy-start.12 = (bf16[302,512]{0,1:T(8,128)(2,1)S(1)}, bf16[302,512]{0,1:T(8,128)(2,1)}, u32[]{:S(2)}) copy-start(bf16[302,512]{0,1:T(8,128)(2,1)} %copy.20) | copy-start | bytes 927748
  1094.3 2.5 copy-start.11
Sparse Core Ops, SparseCore 0:
  10.1 329.8 all-gather.3
  342.6 309.3 all-gather.5
  654.7 309.3 all-gather.7
  994.8 29.5 all-reduce.1
  1102.8 18.7 reduce-scatter.1
where the time goes:
time: 1140 us; the launch traced here: 1130 us
  waiting for transfers between devices  875 us (77%)
  matrix products  157 us (14%)
  local copies, waits for them, and re-layouts  45.9 us (4%)
  other arithmetic  31.7 us (3%)
  between operations  13.8 us (1%)
    all_gather x1, waiting for transfers between devices, local(): lax.all_gather(down_weight, 'seq', axis=0, tiled=True)  312 us
    all_gather x1, waiting for transfers between devices, local(): up_sum = add_rows(lax.all_gather(up_weight, 'seq', axis=0, tiled=True))  297 us
    all_gather x1, waiting for transfers between devices, local(): gate_sum = add_rows(lax.all_gather(gate_weight, 'seq', axis=0, tiled=True))  205 us
    sub x2, matrix products, masked_softmax(): exp_terms = jnp.exp(masked - row_max)  46.2 us
    ppermute x1, waiting for transfers between devices, shifted(): return lax.ppermute(value, axis, pairs)  39.8 us
    dot_general x1, matrix products, local(): lax.dot_general(hidden, lax.all_gather(down_weight, 'seq', axis=0, tiled=...  30.5 us
    dot_general x1, matrix products, local(): jnp.einsum('bhqk,bkhd->bqhd', weights_s, window_values, preferred_element...  24.7 us
  transfers between devices with their start and end apart: 8, of which 5 were waited for; matrix products, arithmetic and copies ran while one was open for 14% of the time, Pallas kernels for 0%

commit v1 on v0

--- a/solution.py
+++ b/solution.py
@@ -9,6 +9,7 @@
 PWIN = 8
 WINDOW = 512
 HALO = 23
+GROUP = 4
 
 
 EPS = 1e-05
@@ -25,6 +26,27 @@
         after = lax.ppermute(first, axis, down)
         value = jnp.concatenate([before, value, after], axis=dim)
     return value
+
+
+def along_far(value, by):
+    if by == 0:
+        return value
+    count = lax.axis_size("seq")
+    plane = count // GROUP
+    pairs = [(i, ((i // plane) ^ by) * plane + i % plane) for i in range(count)]
+    return lax.ppermute(value, "seq", pairs)
+
+
+def along_near(value, by):
+    if by == 0:
+        return value
+    return lax.ppermute(value, "seq", [(i, i ^ by) for i in range(lax.axis_size("seq"))])
+
+
+def along_ffn(value, by):
+    if by == 0:
+        return value
+    return lax.ppermute(value, "ffn", [(i, i ^ by) for i in range(lax.axis_size("ffn"))])
 
 
 def shifted(value, axis, by):
@@ -61,23 +83,99 @@
     cross_out,
     self_out,
 ):
-    patch_count = patches.shape[0]
-    normed = row_normalize(patches).astype(jnp.bfloat16)
-
-    def add_rows(piece_rows):
-        return jnp.dot(normed, piece_rows, preferred_element_type=jnp.float32)
-
-    gate_sum = add_rows(lax.all_gather(gate_weight, "seq", axis=0, tiled=True))
-    up_sum = add_rows(lax.all_gather(up_weight, "seq", axis=0, tiled=True))
-    hidden = (jax.nn.silu(gate_sum) * up_sum).astype(jnp.bfloat16)
+    patch_count, width = patches.shape
+    rows, units = gate_weight.shape
+    ring = lax.axis_size("seq")
+    plane = ring // GROUP
+    cores = lax.axis_size("ffn")
+    seq_at = lax.axis_index("seq")
+    core_at = lax.axis_index("ffn")
+    far, near = seq_at // plane, seq_at % plane
+
+    share = width // cores
+    mine = lax.dynamic_slice_in_dim(patches, core_at * share, share, axis=1)
+    held = jnp.zeros((GROUP * patch_count, share), patches.dtype)
+    for k in range(GROUP):
+        held = lax.dynamic_update_slice_in_dim(
+            held, along_far(mine, k), (far ^ k) * patch_count, axis=0
+        )
+    group = jnp.zeros((GROUP * patch_count, width), patches.dtype)
+    for k in range(cores):
+        group = lax.dynamic_update_slice_in_dim(
+            group, along_ffn(held, k), (core_at ^ k) * share, axis=1
+        )
+    normed = row_normalize(group).astype(jnp.bfloat16)
+    slabs = []
+    for j in range(plane):
+        picked = [
+            lax.dynamic_slice_in_dim(normed, ((far ^ k) * plane + (near ^ j)) * rows, rows, axis=1)
+            for k in range(GROUP)
+        ]
+        slabs.append(jnp.concatenate(picked, axis=1))
+
+    quarter = units // GROUP
+    head = min(quarter, -(-quarter // 256) * 128)
+    pieces = [(0, head), (head, quarter - head)]
+    hidden_all = jnp.zeros((GROUP * patch_count, units), jnp.bfloat16)
+    for at, size in pieces:
+        column = []
+        for k in range(GROUP):
+            start = (far ^ k) * quarter + at
+            both = jnp.concatenate(
+                [
+                    lax.dynamic_slice_in_dim(gate_weight, start, size, axis=1),
+                    lax.dynamic_slice_in_dim(up_weight, start, size, axis=1),
+                ],
+                axis=1,
+            )
+            column.append(along_far(both, k))
+        column = jnp.concatenate(column, axis=0)
+        sums = 0.0
+        for j in range(plane):
+            sums += jnp.dot(
+                slabs[j], along_near(column, j), preferred_element_type=jnp.float32
+            )
+        hidden = (jax.nn.silu(sums[:, :size]) * sums[:, size:]).astype(jnp.bfloat16)
+        for k in range(GROUP):
+            hidden_all = lax.dynamic_update_slice_in_dim(
+                hidden_all, along_far(hidden, k), (far ^ k) * quarter + at, axis=1
+            )
+
+    down = jnp.zeros((plane * rows, units), down_weight.dtype)
+    for j in range(plane):
+        down = lax.dynamic_update_slice_in_dim(
+            down, along_near(down_weight, j), (near ^ j) * rows, axis=0
+        )
     ffn_out = lax.dot_general(
-        hidden,
-        lax.all_gather(down_weight, "seq", axis=0, tiled=True),
-        (((1,), (1,)), ((), ())),
-        preferred_element_type=jnp.float32,
-    )
-    ffn_whole = lax.psum(ffn_out, "ffn")
-    global_out = (patches.astype(jnp.float32) + ffn_whole).astype(jnp.bfloat16)
+        hidden_all, down, (((1,), (1,)), ((), ())), preferred_element_type=jnp.float32
+    )
+    cut = plane * rows // cores
+    ffn_whole = 0.0
+    for k in range(cores):
+        ffn_whole += along_ffn(
+            lax.dynamic_slice_in_dim(ffn_out, (core_at ^ k) * cut, cut, axis=1), k
+        )
+    group_cut = lax.dynamic_slice_in_dim(group, (far * cores + core_at) * cut, cut, axis=1)
+    out_cut = (group_cut.astype(jnp.float32) + ffn_whole).astype(jnp.bfloat16)
+    returned = jnp.concatenate(
+        [
+            along_far(
+                lax.dynamic_slice_in_dim(out_cut, (far ^ k) * patch_count, patch_count, axis=0), k
+            )
+            for k in range(GROUP)
+        ],
+        axis=1,
+    )
+    global_out = jnp.zeros((patch_count, width), jnp.bfloat16)
+    for c in range(cores):
+        other = along_ffn(returned, c)
+        for k in range(GROUP):
+            global_out = lax.dynamic_update_slice_in_dim(
+                global_out,
+                other[:, k * cut : (k + 1) * cut],
+                ((far ^ k) * cores + (core_at ^ c)) * cut,
+                axis=1,
+            )
     head_cols = key_weight.shape[1]
     head_count = head_cols // HD
     score_scale = 1.0 / math.sqrt(HD)
@@ -153,12 +251,15 @@
         "bhqk,bkhd->bqhd", weights_s, window_values, preferred_element_type=jnp.float32
     )
     context_s = context_s.astype(jnp.bfloat16).reshape(byte_count, head_cols)
-    partial_sum = jnp.dot(context_c, cross_out, preferred_element_type=jnp.float32) + jnp.dot(
-        context_s, self_out, preferred_element_type=jnp.float32
-    )
-    return lax.psum_scatter(partial_sum, "ffn", scatter_dimension=1, tiled=True).astype(
-        jnp.bfloat16
-    )
+    out_cols = cross_out.shape[1] // cores
+    total = 0.0
+    for context, weight in ((context_s, self_out), (context_c, cross_out)):
+        for k in range(cores):
+            block = lax.dynamic_slice_in_dim(weight, (core_at ^ k) * out_cols, out_cols, axis=1)
+            total += jnp.dot(
+                along_ffn(context, k), along_ffn(block, k), preferred_element_type=jnp.float32
+            )
+    return total.astype(jnp.bfloat16)
 
 
 def solution(mesh):

time: 1140 us -> 758 us (0.66)
  waiting for transfers between devices: 875 us -> 404 us
  local copies, waits for them, and re-layouts: 45.9 us -> 96.9 us
  starting transfers between devices: 8.7 us -> 49 us
  between operations: 13.8 us -> 1.27 us
  other arithmetic: 31.7 us -> 43.4 us
    all_gather x3 -> x0, waiting for transfers between devices: 814 us -> none  [the longest x1 312 us: local(): lax.all_gather(down_weight, 'seq', axis=0, tiled=True)]
    ppermute x0 -> x34, waiting for transfers between devices: none -> 404 us  [the longest x18 241 us: along_far(): return lax.ppermute(value, 'seq', pairs)]
    ppermute x1, waiting for transfers between devices: 39.8 us -> 0.01 us  [shifted(): return lax.ppermute(value, axis, pairs)]
    ppermute x0 -> x34, starting transfers between devices: none -> 39.8 us  [the longest x18 18.6 us: along_far(): return lax.ppermute(value, 'seq', pairs)]
    dynamic_update_slice x0 -> x23, local copies, waits for them, and re-layouts: none -> 24.6 us  [the longest x4 10 us: local(): lax.dynamic_update_slice_in_dim(down, along_near(down_weight, j), (near ^...]
    reduce_scatter x1 -> x0, waiting for transfers between devices: 18.9 us -> none  [local(): lax.psum_scatter(partial_sum, 'ffn', scatter_dimension=1, tiled=True)]
    dynamic_slice x0 -> x8, local copies, waits for them, and re-layouts: none -> 12.3 us  [the longest x2 4.86 us: local(): lax.dynamic_slice_in_dim(up_weight, start, size, axis=1)]
    concatenate x0 -> x9, other arithmetic: none -> 12 us  [the longest x2 5.94 us: local(): column = jnp.concatenate(column, axis=0)]
  transfers between devices with their start and end apart: 8 -> 37, of which waited for: 5 -> 16; matrix products, arithmetic and copies ran while one was open for 14% -> 37% of each run, Pallas kernels for 0% -> 0%
where the time goes in v1:
time: 758 us; the launch traced here: 747 us
  waiting for transfers between devices  404 us (53%)
  matrix products  152 us (20%)
  local copies, waits for them, and re-layouts  96.9 us (13%)
  starting transfers between devices  49 us (6%)
  other arithmetic  43.4 us (6%)
    ppermute x18, waiting for transfers between devices, along_far(): return lax.ppermute(value, 'seq', pairs)  241 us
    ppermute x9, waiting for transfers between devices, along_near(): lax.ppermute(value, 'seq', [(i, i ^ by) for i in range(lax.axis_size('seq...  161 us
    sub x2, matrix products, masked_softmax(): exp_terms = jnp.exp(masked - row_max)  43.6 us
    dot_general x8, matrix products, local(): jnp.dot(slabs[j], along_near(column, j), preferred_element_type=jnp.float32)  38.6 us
    dot_general x1, matrix products, local(): jnp.einsum('bhqk,bkhd->bqhd', weights_s, window_values, preferred_element...  25 us
    ppermute x18, starting transfers between devices, along_far(): return lax.ppermute(value, 'seq', pairs)  18.6 us
  transfers between devices with their start and end apart: 37, of which 16 were waited for; matrix products, arithmetic and copies ran while one was open for 37% of the time, Pallas kernels for 0%

profile of v1, /device:TPU:23, one launch (start us, length us, event | category | flops | bytes accessed | tf_op | source)
XLA Modules:
  0.0 746.9 jit_solution(17611778559032341686)
XLA Ops:
  6.9 2.4 constant_dynamic-slice_fusion.11
  11.0 4.1 collective-permute-start.17
  15.9 4.9 convolution_convert_fusion.2
  20.7 2.5 constant_dynamic-slice_fusion.31
  24.1 2.6 broadcast_in_dim.34
  27.8 2.4 convolution_convert_fusion.3
  30.2 18.3 %collective-permute-done.3 = bf16[256,2048]{0,1:T(8,128)(2,1)} collective-permute-done((bf16[256,2048]{0,1:T(8,128)(2,1)S(1)}, bf16[256,2048]{0,1:T(8,128)(2,1)}, u32[]{:S(2)}, u32[]{:S(2)}) %collective-permute-start.3) | collective-permute-done | bytes 1048608 | tf_op jit(solution)/shard_map/ppermute | solution.py:37
  50.8 2.4 constant_dynamic-update-slice_fusion.20
  53.4 2.4 constant_dynamic-update-slice_fusion.19
  55.8 57.8 %collective-permute-done.5 = bf16[256,2048]{0,1:T(8,128)(2,1)} collective-permute-done((bf16[256,2048]{0,1:T(8,128)(2,1)S(1)}, bf16[256,2048]{0,1:T(8,128)(2,1)}, u32[]{:S(2)}, u32[]{:S(2)}) %collective-permute-start.5) | collective-permute-done | bytes 1048608 | tf_op jit(solution)/shard_map/ppermute | solution.py:37
  116.0 3.2 collective-permute-start.6
  120.8 2.4 broadcast_and_fusion
  123.2 3.7 convolution_convert_fusion.1
  128.6 3.4 broadcast.147.clone.1
  132.0 2.9 constant_dynamic-update-slice_fusion.7
  135.1 4.6 collective-permute-done.17
  139.7 3.1 collective-permute-start.8
  142.9 6.2 reshape.197
  149.2 2.5 pad_maximum_fusion.8
  151.7 12.5 %collective-permute-done.9 = bf16[256,1024]{1,0:T(8,128)(2,1)} collective-permute-done((bf16[256,1024]{1,0:T(8,128)(2,1)}, bf16[256,1024]{1,0:T(8,128)(2,1)}, u32[]{:S(2)}, u32[]{:S(2)}) %collective-permute-start.9) | collective-permute-done | bytes 524320 | tf_op jit(solution)/shard_map/ppermute | solution.py:37
  164.4 9.0 %collective-permute-done.8 = bf16[256,1024]{1,0:T(8,128)(2,1)} collective-permute-done((bf16[256,1024]{1,0:T(8,128)(2,1)}, bf16[256,1024]{1,0:T(8,128)(2,1)}, u32[]{:S(2)}, u32[]{:S(2)}) %collective-permute-start.8) | collective-permute-done | bytes 524320 | tf_op jit(solution)/shard_map/ppermute | solution.py:37
  173.6 3.5 pad_maximum_fusion.4
  179.4 2.7 constant_dynamic-update-slice_fusion.17
  183.4 2.9 constant_dynamic-update-slice_fusion.6
  186.5 2.7 constant_dynamic-update-slice_fusion.16
  192.6 9.2 %fusion.10 = bf16[1024,4096]{0,1:T(8,128)(2,1)} fusion(bf16[1024,4096]{0,1:T(8,128)(2,1)} %copy-done.2, f32[1024]{0:T(1024)S(1)} %add_rsqrt_fusion), kind=kLoop, calls=%fused_computation.17 | loop fusion | flops 12582912 | bytes 16781312 | tf_op jit(solution)/shard_map/convert_element_type | solution.py:107
  201.8 4.6 constant_dynamic-slice_fusion.16
  206.4 125.5 %collective-permute-done.11 = bf16[1024,1024]{1,0:T(8,128)(2,1)} collective-permute-done((bf16[1024,1024]{1,0:T(8,128)(2,1)S(1)}, bf16[1024,1024]{1,0:T(8,128)(2,1)}, u32[]{:S(2)}, u32[]{:S(2)}) %collective-permute-start.11) | collective-permute-done | bytes 2097184 | tf_op jit(solution)/shard_map/ppermute | solution.py:43
  332.2 4.0 fusion.35
  336.2 3.8 fusion.39
  340.4 6.2 fusion.37
  348.8 5.1 add_add_fusion
  355.1 9.7 %collective-permute-done.20 = bf16[1024,768]{1,0:T(8,128)(2,1)} collective-permute-done((bf16[1024,768]{1,0:T(8,128)(2,1)S(1)}, bf16[1024,768]{1,0:T(8,128)(2,1)}, u32[]{:S(2)}, u32[]{:S(2)}) %collective-permute-start.20) | collective-permute-done | bytes 1572896 | tf_op jit(solution)/shard_map/ppermute | solution.py:43
  364.8 4.9 fusion.34
  371.1 4.9 fusion.36
  376.1 5.0 fusion.38
  381.0 24.4 %collective-permute-done.21 = bf16[1024,768]{1,0:T(8,128)(2,1)} collective-permute-done((bf16[1024,768]{1,0:T(8,128)(2,1)S(1)}, bf16[1024,768]{1,0:T(8,128)(2,1)}, u32[]{:S(2)}, u32[]{:S(2)}) %collective-permute-start.21) | collective-permute-done | bytes 1572896 | tf_op jit(solution)/shard_map/ppermute | solution.py:43
  405.6 4.7 add_add_fusion.1
  412.7 43.8 %collective-permute-done.15 = bf16[1024,512]{1,0:T(8,128)(2,1)S(1)} collective-permute-done((bf16[1024,512]{1,0:T(8,128)(2,1)S(1)}, bf16[1024,512]{1,0:T(8,128)(2,1)S(1)}, u32[]{:S(2)}, u32[]{:S(2)}) %collective-permute-start.15) | collective-permute-done | bytes 1048608 | tf_op jit(solution)/shard_map/ppermute | solution.py:37
  457.2 3.4 collective-permute-start.23
  461.9 2.9 constant_dynamic-update-slice_fusion.4
  464.8 3.5 collective-permute-done.22
  468.5 24.4 %collective-permute-done.23 = bf16[1024,384]{1,0:T(8,128)(2,1)S(1)} collective-permute-done((bf16[1024,384]{1,0:T(8,128)(2,1)S(1)}, bf16[1024,384]{1,0:T(8,128)(2,1)S(1)}, u32[]{:S(2)}, u32[]{:S(2)}) %collective-permute-start.23) | collective-permute-done | bytes 786464 | tf_op jit(solution)/shard_map/ppermute | solution.py:37
  493.1 52.7 %collective-permute-done.24 = bf16[1024,384]{1,0:T(8,128)(2,1)S(1)} collective-permute-done((bf16[1024,384]{1,0:T(8,128)(2,1)S(1)}, bf16[1024,384]{1,0:T(8,128)(2,1)S(1)}, u32[]{:S(2)}, u32[]{:S(2)}) %collective-permute-start.24) | collective-permute-done | bytes 786464 | tf_op jit(solution)/shard_map/ppermute | solution.py:37
  546.0 10.1 %fusion.67 = f32[1024,1024]{0,1:T(8,128)S(1)} fusion(bf16[1024,3584]{1,0:T(8,128)(2,1)S(1)} %constant_dynamic-update-slice_fusion.8, bf16[1024,3584]{1,0:T(8,128)(2,1)} %constant_dynamic-update-slice_fusion.4), kind=kOutput, calls=%fused_computation.176 | convolution fusion | flops 7516192768 | bytes 18874368 | tf_op jit(solution)/shard_map/dot_general | solution.py:149
  557.6 8.2 %collective-permute-start.28 = (f32[1024,512]{0,1:T(8,128)}, f32[1024,512]{0,1:T(8,128)}, u32[]{:S(2)}, u32[]{:S(2)}) collective-permute-start(f32[1024,512]{0,1:T(8,128)} %constant_dynamic-slice_fusion.4), channel_id=1, source_target_pairs={{0,1},{1,0},{2,3},{3,2},{4,5},{5,4},{6,7},{7,6},{8,9},{9,8},{10,11... | collective-permute-start | bytes 6291464 | tf_op jit(solution)/shard_map/ppermute | solution.py:49
  567.2 3.8 convolution_convert_fusion
  571.0 11.1 %pad_maximum_fusion = (bf16[2048,1024]{0,1:T(8,128)(2,1)}, bf16[2048,1024]{0,1:T(8,128)(2,1)}) fusion(bf16[2048,512]{0,1:T(8,128)(2,1)S(1)} %convolution_convert_fusion.2, bf16[2048,512]{0,1:T(8,128)(2,1)S(1)} %copy-done.5, bf16[512,1024]{0,1:T(8,128)(2,1)S(1)} %collective-permute-done), kind=kLoop, calls=%fused_computation.24 | loop fusion | flops 20971520 | bytes 13631488 | tf_op jit(solution)/shard_map/concatenate | solution.py:221
  582.1 7.8 %reshape.187 = bf16[4,512,1024]{1,0,2:T(4,128)(2,1)} reshape(bf16[2048,1024]{0,1:T(8,128)(2,1)} %get-tuple-element.30) | data formatting | bytes 8388608 | tf_op jit(solution)/shard_map/reshape | solution.py:226
  589.9 8.3 %reshape.188 = bf16[4,512,1024]{1,0,2:T(4,128)(2,1)} reshape(bf16[2048,1024]{0,1:T(8,128)(2,1)} %get-tuple-element.29) | data formatting | bytes 8388608 | tf_op jit(solution)/shard_map/reshape | solution.py:227
  598.2 3.8 constant_dynamic-update-slice_fusion.23
  604.2 2.5 add_convert_fusion.1
  609.7 4.2 fusion.58
  614.0 3.5 copy.23
  617.9 13.8 %collective-permute-done.31 = bf16[256,512]{0,1:T(8,128)(2,1)S(1)} collective-permute-done((bf16[256,512]{0,1:T(8,128)(2,1)S(1)}, bf16[256,512]{0,1:T(8,128)(2,1)S(1)}, u32[]{:S(2)}, u32[]{:S(2)}) %collective-permute-start.31) | collective-permute-done | bytes 262176 | tf_op jit(solution)/shard_map/ppermute | solution.py:37
  635.0 30.6 %fusion.61 = (f32[4,8,512]{2,1,0:T(8,128)S(1)}, f32[4,8,512,1024]{3,2,1,0:T(8,128)}) fusion(pred[4,512,1024]{2,1,0:T(8,128)(4,1)S(1)} %copy-done.8, bf16[4,1024,8,64]{1,3,2,0:T(8,128)(2,1)} %bitcast.57, bf16[4,512,8,64]{3,2,1,0:T(8,128)(2,1)} %reshape.197), kind=kOutput, calls=%fused_computation.174 | convolution fusion | flops 2214593536 | bytes 75563008 | tf_op jit(solution)/shard_map/sub | solution.py:66
  665.6 5.7 copy.21
  677.1 5.2 collective-permute-start.33
  682.2 25.0 %convert_bitcast_fusion = bf16[4,512,8,64]{1,3,2,0:T(8,128)(2,1)S(1)} fusion(bf16[4,1024,8,64]{1,3,2,0:T(8,128)(2,1)} %bitcast.56, f32[4,8,512,1024]{3,2,1,0:T(8,128)} %get-tuple-element.59, f32[4,8,512]{2,1,0:T(8,128)S(1)} %get-tuple-element.58), kind=kOutput, calls=%fused_computation.49 | convolution fusion | flops 2182086656 | bytes 73465856 | tf_op jit(solution)/shard_map/bhqk,bkhd->bqhd/dot_general | solution.py:250
  712.2 13.0 %fusion.60 = (f32[8,2048]{1,0:T(8,128)S(1)}, f32[8,2048,302]{1,2,0:T(8,128)}) fusion(pred[2048,302]{0,1:T(8,128)(4,1)S(1)} %copy-done.26, bf16[2048,8,64]{0,2,1:T(8,128)(2,1)} %bitcast.62, bf16[302,8,64]{0,2,1:T(8,128)(2,1)} %bitcast.61), kind=kOutput, calls=%fused_computation.173 | convolution fusion | flops 653132096 | bytes 22882304 | tf_op jit(solution)/shard_map/sub | solution.py:66
  725.2 9.0 %fusion.23 = bf16[8,64,2048]{2,1,0:T(8,128)(2,1)S(1)} fusion(bf16[302,8,64]{0,2,1:T(8,128)(2,1)S(1)} %bitcast.60, f32[8,2048,302]{1,2,0:T(8,128)} %get-tuple-element.57, f32[8,2048]{1,0:T(8,128)S(1)} %get-tuple-element.56), kind=kOutput, calls=%fused_computation.39 | convolution fusion | flops 644284416 | bytes 22263808 | tf_op jit(solution)/shard_map/hqk,khd->qhd/dot_general | solution.py:217
  736.3 2.8 collective-permute-done.2
  739.1 2.9 fusion.66
  743.4 3.0 add_convert_fusion
  (193 shorter events, 63.7 us)
Async XLA Ops:
  4.2 44.3 %collective-permute-start.3 = (bf16[256,2048]{0,1:T(8,128)(2,1)S(1)}, bf16[256,2048]{0,1:T(8,128)(2,1)}, u32[]{:S(2)}, u32[]{:S(2)}) collective-permute-start(bf16[256,2048]{0,1:T(8,128)(2,1)S(1)} %copy.31), channel_id=1, source_target_pairs={{0,8},{2,10},{4,12},{6,14},{8,0},{10,2},{12,4},{14,6},{16,24},{18,... | collective-permute-start | bytes 3145736 | tf_op jit(solution)/shard_map/ppermute | solution.py:37
  5.5 47.7 %collective-permute-start.4 = (bf16[256,2048]{0,1:T(8,128)(2,1)S(1)}, bf16[256,2048]{0,1:T(8,128)(2,1)}, u32[]{:S(2)}, u32[]{:S(2)}) collective-permute-start(bf16[256,2048]{0,1:T(8,128)(2,1)S(1)} %copy.31), channel_id=1, source_target_pairs={{0,16},{2,18},{4,20},{6,22},{8,24},{10,26},{12,28},{14,30},{16,0},... | collective-permute-start | bytes 3145736 | tf_op jit(solution)/shard_map/ppermute | solution.py:37
  5.6 108.0 %collective-permute-start.5 = (bf16[256,2048]{0,1:T(8,128)(2,1)S(1)}, bf16[256,2048]{0,1:T(8,128)(2,1)}, u32[]{:S(2)}, u32[]{:S(2)}) collective-permute-start(bf16[256,2048]{0,1:T(8,128)(2,1)S(1)} %copy.31), channel_id=1, source_target_pairs={{0,24},{2,26},{4,28},{6,30},{8,16},{10,18},{12,20},{14,22},{16,8},... | collective-permute-start | bytes 3145736 | tf_op jit(solution)/shard_map/ppermute | solution.py:37
  10.0 124.8 %collective-permute-start.18 = (bf16[256,768]{1,0:T(8,128)(2,1)}, bf16[256,768]{1,0:T(8,128)(2,1)}, u32[]{:S(2)}, u32[]{:S(2)}) collective-permute-start(bf16[256,768]{1,0:T(8,128)(2,1)} %pad_maximum_fusion.16), channel_id=1, source_target_pairs={{0,24},{2,26},{4,28},{6,30},{8,16},{10,18},{12,20},{14,22},{16,8},... | collective-permute-start | bytes 1179656 | tf_op jit(solution)/shard_map/ppermute | solution.py:37
  11.0 128.7 %collective-permute-start.17 = (bf16[256,768]{1,0:T(8,128)(2,1)}, bf16[256,768]{1,0:T(8,128)(2,1)}, u32[]{:S(2)}, u32[]{:S(2)}) collective-permute-start(bf16[256,768]{1,0:T(8,128)(2,1)} %pad_maximum_fusion.15), channel_id=1, source_target_pairs={{0,16},{2,18},{4,20},{6,22},{8,24},{10,26},{12,28},{14,30},{16,0},... | collective-permute-start | bytes 1179656 | tf_op jit(solution)/shard_map/ppermute | solution.py:37
  23.2 4.6 copy-start.37
  30.2 90.1 %copy-start.4 = (bf16[2048,512]{0,1:T(8,128)(2,1)}, bf16[2048,512]{0,1:T(8,128)(2,1)S(1)}, u32[]{:S(2)}) copy-start(bf16[2048,512]{0,1:T(8,128)(2,1)S(1)} %convolution_convert_fusion.3) | copy-start | bytes 6291460
  48.5 94.3 %collective-permute-start.16 = (bf16[256,768]{1,0:T(8,128)(2,1)}, bf16[256,768]{1,0:T(8,128)(2,1)}, u32[]{:S(2)}, u32[]{:S(2)}) collective-permute-start(bf16[256,768]{1,0:T(8,128)(2,1)} %pad_maximum_fusion.14), channel_id=1, source_target_pairs={{0,8},{2,10},{4,12},{6,14},{8,0},{10,2},{12,4},{14,6},{16,24},{18,... | collective-permute-start | bytes 1179656 | tf_op jit(solution)/shard_map/ppermute | solution.py:37
  53.2 129.0 %collective-permute-start.25 = (bf16[256,3584]{1,0:T(8,128)(2,1)}, bf16[256,3584]{1,0:T(8,128)(2,1)}, u32[]{:S(2)}, u32[]{:S(2)}) collective-permute-start(bf16[256,3584]{1,0:T(8,128)(2,1)} %param.17), channel_id=1, source_target_pairs={{0,2},{2,0},{4,6},{6,4},{8,10},{10,8},{12,14},{14,12},{16,18},{18,... | collective-permute-start | bytes 5505032 | tf_op jit(solution)/shard_map/ppermute | solution.py:43
  116.0 70.4 %collective-permute-start.6 = (bf16[1024,2048]{0,1:T(8,128)(2,1)}, bf16[1024,2048]{0,1:T(8,128)(2,1)}, u32[]{:S(2)}, u32[]{:S(2)}) collective-permute-start(bf16[1024,2048]{0,1:T(8,128)(2,1)} %constant_dynamic-update-slice_fusion.18), channel_id=1, source_target_pairs={{0,1},{1,0},{2,3},{3,2},{4,5},{5,4},{6,7},{7,6},{8,9},{9,8},{10,11... | collective-permute-start | bytes 12582920 | tf_op jit(solution)/shard_map/ppermute | solution.py:49
  134.9 14.3 %copy-start.32 = (s32[2048]{0:T(1024)S(1)}, s32[2048]{0:T(1024)}, u32[]{:S(2)}) copy-start(s32[2048]{0:T(1024)} %param.21) | copy-start | bytes 24580
  134.9 14.3 %copy-start.22 = (bf16[256,384]{1,0:T(8,128)(2,1)S(1)}, bf16[256,384]{1,0:T(8,128)(2,1)}, u32[]{:S(2)}) copy-start(bf16[256,384]{1,0:T(8,128)(2,1)} %get-tuple-element.35) | copy-start | bytes 589828
  134.9 14.3 %copy-start.24 = (bf16[256,384]{1,0:T(8,128)(2,1)S(1)}, bf16[256,384]{1,0:T(8,128)(2,1)}, u32[]{:S(2)}) copy-start(bf16[256,384]{1,0:T(8,128)(2,1)} %get-tuple-element.67) | copy-start | bytes 589828
  134.9 29.3 %collective-permute-start.9 = (bf16[256,1024]{1,0:T(8,128)(2,1)}, bf16[256,1024]{1,0:T(8,128)(2,1)}, u32[]{:S(2)}, u32[]{:S(2)}) collective-permute-start(bf16[256,1024]{1,0:T(8,128)(2,1)} %pad_maximum_fusion.13), channel_id=1, source_target_pairs={{0,24},{2,26},{4,28},{6,30},{8,16},{10,18},{12,20},{14,22},{16,8},... | collective-permute-start | bytes 1572872 | tf_op jit(solution)/shard_map/ppermute | solution.py:37
  139.7 33.7 %collective-permute-start.8 = (bf16[256,1024]{1,0:T(8,128)(2,1)}, bf16[256,1024]{1,0:T(8,128)(2,1)}, u32[]{:S(2)}, u32[]{:S(2)}) collective-permute-start(bf16[256,1024]{1,0:T(8,128)(2,1)} %pad_maximum_fusion.12), channel_id=1, source_target_pairs={{0,16},{2,18},{4,20},{6,22},{8,24},{10,26},{12,28},{14,30},{16,0},... | collective-permute-start | bytes 1572872 | tf_op jit(solution)/shard_map/ppermute | solution.py:37
  142.8 30.8 %collective-permute-start.7 = (bf16[256,1024]{1,0:T(8,128)(2,1)}, bf16[256,1024]{1,0:T(8,128)(2,1)}, u32[]{:S(2)}, u32[]{:S(2)}) collective-permute-start(bf16[256,1024]{1,0:T(8,128)(2,1)} %pad_maximum_fusion.11), channel_id=1, source_target_pairs={{0,8},{2,10},{4,12},{6,14},{8,0},{10,2},{12,4},{14,6},{16,24},{18,... | collective-permute-start | bytes 1572872 | tf_op jit(solution)/shard_map/ppermute | solution.py:37
  142.9 30.6 %copy-start.17 = (bf16[256,512]{1,0:T(8,128)(2,1)S(1)}, bf16[256,512]{1,0:T(8,128)(2,1)}, u32[]{:S(2)}) copy-start(bf16[256,512]{1,0:T(8,128)(2,1)} %get-tuple-element.63) | copy-start | bytes 786436
  164.2 296.4 %collective-permute-start.26 = (bf16[256,3584]{1,0:T(8,128)(2,1)}, bf16[256,3584]{1,0:T(8,128)(2,1)S(1)}, u32[]{:S(2)}, u32[]{:S(2)}) collective-permute-start(bf16[256,3584]{1,0:T(8,128)(2,1)} %param.17), channel_id=1, source_target_pairs={{0,4},{2,6},{4,0},{6,2},{8,12},{10,14},{12,8},{14,10},{16,20},{18,... | collective-permute-start | bytes 5505032 | tf_op jit(solution)/shard_map/ppermute | solution.py:43
  173.4 288.6 %collective-permute-start.27 = (bf16[256,3584]{1,0:T(8,128)(2,1)}, bf16[256,3584]{1,0:T(8,128)(2,1)}, u32[]{:S(2)}, u32[]{:S(2)}) collective-permute-start(bf16[256,3584]{1,0:T(8,128)(2,1)} %param.17), channel_id=1, source_target_pairs={{0,6},{2,4},{4,2},{6,0},{8,14},{10,12},{12,10},{14,8},{16,22},{18,... | collective-permute-start | bytes 5505032 | tf_op jit(solution)/shard_map/ppermute | solution.py:43
  177.0 154.9 %collective-permute-start.11 = (bf16[1024,1024]{1,0:T(8,128)(2,1)S(1)}, bf16[1024,1024]{1,0:T(8,128)(2,1)}, u32[]{:S(2)}, u32[]{:S(2)}) collective-permute-start(bf16[1024,1024]{1,0:T(8,128)(2,1)S(1)} %pad_maximum_fusion.4), channel_id=1, source_target_pairs={{0,4},{2,6},{4,0},{6,2},{8,12},{10,14},{12,8},{14,10},{16,20},{18,... | collective-permute-start | bytes 6291464 | tf_op jit(solution)/shard_map/ppermute | solution.py:43
  182.2 157.9 %collective-permute-start.10 = (bf16[1024,1024]{1,0:T(8,128)(2,1)S(1)}, bf16[1024,1024]{1,0:T(8,128)(2,1)}, u32[]{:S(2)}, u32[]{:S(2)}) collective-permute-start(bf16[1024,1024]{1,0:T(8,128)(2,1)S(1)} %pad_maximum_fusion.4), channel_id=1, source_target_pairs={{0,2},{2,0},{4,6},{6,4},{8,10},{10,8},{12,14},{14,12},{16,18},{18,... | collective-permute-start | bytes 6291464 | tf_op jit(solution)/shard_map/ppermute | solution.py:43
  186.3 160.3 %collective-permute-start.12 = (bf16[1024,1024]{1,0:T(8,128)(2,1)S(1)}, bf16[1024,1024]{1,0:T(8,128)(2,1)}, u32[]{:S(2)}, u32[]{:S(2)}) collective-permute-start(bf16[1024,1024]{1,0:T(8,128)(2,1)S(1)} %pad_maximum_fusion.4), channel_id=1, source_target_pairs={{0,6},{2,4},{4,2},{6,0},{8,14},{10,12},{12,10},{14,8},{16,22},{18,... | collective-permute-start | bytes 6291464 | tf_op jit(solution)/shard_map/ppermute | solution.py:43
  201.8 130.2 %copy-start.11 = (bf16[1024,768]{1,0:T(8,128)(2,1)S(1)}, bf16[1024,768]{1,0:T(8,128)(2,1)}, u32[]{:S(2)}) copy-start(bf16[1024,768]{1,0:T(8,128)(2,1)} %pad_maximum_fusion.8) | copy-start | bytes 4718596
  206.4 129.8 %copy-start.27 = (bf16[1024,256]{0,1:T(8,128)(2,1)}, bf16[1024,256]{0,1:T(8,128)(2,1)S(1)}, u32[]{:S(2)}) copy-start(bf16[1024,256]{0,1:T(8,128)(2,1)S(1)} %get-tuple-element.19) | copy-start | bytes 1572868
  206.4 129.8 %copy-start.29 = (bf16[1024,256]{0,1:T(8,128)(2,1)}, bf16[1024,256]{0,1:T(8,128)(2,1)S(1)}, u32[]{:S(2)}) copy-start(bf16[1024,256]{0,1:T(8,128)(2,1)S(1)} %get-tuple-element.20) | copy-start | bytes 1572868
  332.0 32.8 %collective-permute-start.20 = (bf16[1024,768]{1,0:T(8,128)(2,1)S(1)}, bf16[1024,768]{1,0:T(8,128)(2,1)}, u32[]{:S(2)}, u32[]{:S(2)}) collective-permute-start(bf16[1024,768]{1,0:T(8,128)(2,1)S(1)} %copy-done.11), channel_id=1, source_target_pairs={{0,4},{2,6},{4,0},{6,2},{8,12},{10,14},{12,8},{14,10},{16,20},{18,... | collective-permute-start | bytes 4718600 | tf_op jit(solution)/shard_map/ppermute | solution.py:43
  340.1 30.7 %collective-permute-start.19 = (bf16[1024,768]{1,0:T(8,128)(2,1)S(1)}, bf16[1024,768]{1,0:T(8,128)(2,1)}, u32[]{:S(2)}, u32[]{:S(2)}) collective-permute-start(bf16[1024,768]{1,0:T(8,128)(2,1)S(1)} %copy-done.11), channel_id=1, source_target_pairs={{0,2},{2,0},{4,6},{6,4},{8,10},{10,8},{12,14},{14,12},{16,18},{18,... | collective-permute-start | bytes 4718600 | tf_op jit(solution)/shard_map/ppermute | solution.py:43
  346.6 58.8 %collective-permute-start.21 = (bf16[1024,768]{1,0:T(8,128)(2,1)S(1)}, bf16[1024,768]{1,0:T(8,128)(2,1)}, u32[]{:S(2)}, u32[]{:S(2)}) collective-permute-start(bf16[1024,768]{1,0:T(8,128)(2,1)S(1)} %copy-done.11), channel_id=1, source_target_pairs={{0,6},{2,4},{4,2},{6,0},{8,14},{10,12},{12,10},{14,8},{16,22},{18,... | collective-permute-start | bytes 4718600 | tf_op jit(solution)/shard_map/ppermute | solution.py:43
  354.4 10.5 %copy-start.28 = (bf16[1024,256]{0,1:T(8,128)(2,1)S(1)}, bf16[1024,256]{0,1:T(8,128)(2,1)}, u32[]{:S(2)}) copy-start(bf16[1024,256]{0,1:T(8,128)(2,1)} %copy-done.27) | copy-start | bytes 1572868
  354.4 10.5 %copy-start.30 = (bf16[1024,256]{0,1:T(8,128)(2,1)S(1)}, bf16[1024,256]{0,1:T(8,128)(2,1)}, u32[]{:S(2)}) copy-start(bf16[1024,256]{0,1:T(8,128)(2,1)} %copy-done.29) | copy-start | bytes 1572868
  364.8 45.5 %collective-permute-start.13 = (bf16[1024,512]{1,0:T(8,128)(2,1)S(1)}, bf16[1024,512]{1,0:T(8,128)(2,1)S(1)}, u32[]{:S(2)}, u32[]{:S(2)}) collective-permute-start(bf16[1024,512]{1,0:T(8,128)(2,1)S(1)} %get-tuple-element.10), channel_id=1, source_target_pairs={{0,8},{2,10},{4,12},{6,14},{8,0},{10,2},{12,4},{14,6},{16,24},{18,... | collective-permute-start | bytes 3145736 | tf_op jit(solution)/shard_map/ppermute | solution.py:37
  369.7 6.3 copy-start.23
  369.7 6.3 copy-start.25
  370.8 41.8 %collective-permute-start.14 = (bf16[1024,512]{1,0:T(8,128)(2,1)S(1)}, bf16[1024,512]{1,0:T(8,128)(2,1)S(1)}, u32[]{:S(2)}, u32[]{:S(2)}) collective-permute-start(bf16[1024,512]{1,0:T(8,128)(2,1)S(1)} %get-tuple-element.10), channel_id=1, source_target_pairs={{0,16},{2,18},{4,20},{6,22},{8,24},{10,26},{12,28},{14,30},{16,0},... | collective-permute-start | bytes 3145736 | tf_op jit(solution)/shard_map/ppermute | solution.py:37
  376.1 29.6 %copy-start.40 = (f32[1024,768]{1,0:T(8,128)S(1)}, f32[1024,768]{1,0:T(8,128)}, u32[]{:S(2)}) copy-start(f32[1024,768]{1,0:T(8,128)} %fusion.34) | copy-start | bytes 9437188
  381.0 29.3 %copy-start.12 = (bf16[512,1024]{0,1:T(8,128)(2,1)S(1)}, bf16[512,1024]{0,1:T(8,128)(2,1)}, u32[]{:S(2)}) copy-start(bf16[512,1024]{0,1:T(8,128)(2,1)} %fusion.27) | copy-start | bytes 3145732
  405.4 51.0 %collective-permute-start.15 = (bf16[1024,512]{1,0:T(8,128)(2,1)S(1)}, bf16[1024,512]{1,0:T(8,128)(2,1)S(1)}, u32[]{:S(2)}, u32[]{:S(2)}) collective-permute-start(bf16[1024,512]{1,0:T(8,128)(2,1)S(1)} %get-tuple-element.10), channel_id=1, source_target_pairs={{0,24},{2,26},{4,28},{6,30},{8,16},{10,18},{12,20},{14,22},{16,8},... | collective-permute-start | bytes 3145736 | tf_op jit(solution)/shard_map/ppermute | solution.py:37
  410.3 160.7 %collective-permute-start = (bf16[512,1024]{0,1:T(8,128)(2,1)S(1)}, bf16[512,1024]{0,1:T(8,128)(2,1)S(1)}, u32[]{:S(2)}, u32[]{:S(2)}) collective-permute-start(bf16[512,1024]{0,1:T(8,128)(2,1)S(1)} %copy-done.12), channel_id=1, source_target_pairs={{0,2},{2,4},{4,6},{6,8},{8,10},{10,12},{12,14},{14,16},{16,18},{18... | collective-permute-start | bytes 3145736 | tf_op jit(solution)/shard_map/ppermute | solution.py:55
  457.1 11.2 %collective-permute-start.22 = (bf16[1024,384]{1,0:T(8,128)(2,1)S(1)}, bf16[1024,384]{1,0:T(8,128)(2,1)S(1)}, u32[]{:S(2)}, u32[]{:S(2)}) collective-permute-start(bf16[1024,384]{1,0:T(8,128)(2,1)S(1)} %get-tuple-element.8), channel_id=1, source_target_pairs={{0,8},{2,10},{4,12},{6,14},{8,0},{10,2},{12,4},{14,6},{16,24},{18,... | collective-permute-start | bytes 2359304 | tf_op jit(solution)/shard_map/ppermute | solution.py:37
  457.2 35.7 %collective-permute-start.23 = (bf16[1024,384]{1,0:T(8,128)(2,1)S(1)}, bf16[1024,384]{1,0:T(8,128)(2,1)S(1)}, u32[]{:S(2)}, u32[]{:S(2)}) collective-permute-start(bf16[1024,384]{1,0:T(8,128)(2,1)S(1)} %get-tuple-element.8), channel_id=1, source_target_pairs={{0,16},{2,18},{4,20},{6,22},{8,24},{10,26},{12,28},{14,30},{16,0},... | collective-permute-start | bytes 2359304 | tf_op jit(solution)/shard_map/ppermute | solution.py:37
  460.6 85.2 %collective-permute-start.24 = (bf16[1024,384]{1,0:T(8,128)(2,1)S(1)}, bf16[1024,384]{1,0:T(8,128)(2,1)S(1)}, u32[]{:S(2)}, u32[]{:S(2)}) collective-permute-start(bf16[1024,384]{1,0:T(8,128)(2,1)S(1)} %get-tuple-element.8), channel_id=1, source_target_pairs={{0,24},{2,26},{4,28},{6,30},{8,16},{10,18},{12,20},{14,22},{16,8},... | collective-permute-start | bytes 2359304 | tf_op jit(solution)/shard_map/ppermute | solution.py:37
  545.9 21.3 %copy-start.39 = (bf16[1024,512]{1,0:T(8,128)(2,1)S(1)}, bf16[1024,512]{1,0:T(8,128)(2,1)}, u32[]{:S(2)}) copy-start(bf16[1024,512]{1,0:T(8,128)(2,1)} %param.22) | copy-start | bytes 3145732
  556.1 14.9 %copy-start.6 = (f32[1024,1024]{0,1:T(8,128)}, f32[1024,1024]{0,1:T(8,128)S(1)}, u32[]{:S(2)}) copy-start(f32[1024,1024]{0,1:T(8,128)S(1)} %fusion.67) | copy-start | bytes 12582916
  556.1 11.1 %copy-start.34 = (bf16[2048,1024]{1,0:T(8,128)(2,1)S(1)}, bf16[2048,1024]{1,0:T(8,128)(2,1)}, u32[]{:S(2)}) copy-start(bf16[2048,1024]{1,0:T(8,128)(2,1)} %param.20) | copy-start | bytes 12582916
  557.6 46.2 %collective-permute-start.28 = (f32[1024,512]{0,1:T(8,128)}, f32[1024,512]{0,1:T(8,128)}, u32[]{:S(2)}, u32[]{:S(2)}) collective-permute-start(f32[1024,512]{0,1:T(8,128)} %constant_dynamic-slice_fusion.4), channel_id=1, source_target_pairs={{0,1},{1,0},{2,3},{3,2},{4,5},{5,4},{6,7},{7,6},{8,9},{9,8},{10,11... | collective-permute-start | bytes 6291464 | tf_op jit(solution)/shard_map/ppermute | solution.py:49
  607.0 10.5 %collective-permute-start.29 = (bf16[256,512]{0,1:T(8,128)(2,1)S(1)}, bf16[256,512]{0,1:T(8,128)(2,1)S(1)}, u32[]{:S(2)}, u32[]{:S(2)}) collective-permute-start(bf16[256,512]{0,1:T(8,128)(2,1)S(1)} %get-tuple-element.49), channel_id=1, source_target_pairs={{0,8},{2,10},{4,12},{6,14},{8,0},{10,2},{12,4},{14,6},{16,24},{18,... | collective-permute-start | bytes 786440 | tf_op jit(solution)/shard_map/ppermute | solution.py:37
  607.1 10.8 %collective-permute-start.30 = (bf16[256,512]{0,1:T(8,128)(2,1)S(1)}, bf16[256,512]{0,1:T(8,128)(2,1)S(1)}, u32[]{:S(2)}, u32[]{:S(2)}) collective-permute-start(bf16[256,512]{0,1:T(8,128)(2,1)S(1)} %get-tuple-element.48), channel_id=1, source_target_pairs={{0,16},{2,18},{4,20},{6,22},{8,24},{10,26},{12,28},{14,30},{16,0},... | collective-permute-start | bytes 786440 | tf_op jit(solution)/shard_map/ppermute | solution.py:37
  608.3 23.3 %collective-permute-start.31 = (bf16[256,512]{0,1:T(8,128)(2,1)S(1)}, bf16[256,512]{0,1:T(8,128)(2,1)S(1)}, u32[]{:S(2)}, u32[]{:S(2)}) collective-permute-start(bf16[256,512]{0,1:T(8,128)(2,1)S(1)} %get-tuple-element.47), channel_id=1, source_target_pairs={{0,24},{2,26},{4,28},{6,30},{8,16},{10,18},{12,20},{14,22},{16,8},... | collective-permute-start | bytes 786440 | tf_op jit(solution)/shard_map/ppermute | solution.py:37
  614.0 21.0 %copy-start.8 = (pred[4,512,1024]{2,1,0:T(8,128)(4,1)S(1)}, pred[4,512,1024]{2,1,0:T(8,128)(4,1)}, u32[]{:S(2)}) copy-start(pred[4,512,1024]{2,1,0:T(8,128)(4,1)} %broadcast_and_fusion) | copy-start | bytes 6291460
  617.9 14.9 %copy-start.13 = (bf16[256,512]{0,1:T(8,128)(2,1)}, bf16[256,512]{0,1:T(8,128)(2,1)S(1)}, u32[]{:S(2)}) copy-start(bf16[256,512]{0,1:T(8,128)(2,1)S(1)} %collective-permute-done.30) | copy-start | bytes 786436
  632.7 38.8 %collective-permute-start.32 = (bf16[256,2048]{0,1:T(8,128)(2,1)}, bf16[256,2048]{0,1:T(8,128)(2,1)S(1)}, u32[]{:S(2)}, u32[]{:S(2)}) collective-permute-start(bf16[256,2048]{0,1:T(8,128)(2,1)} %pad_maximum_fusion.9), channel_id=1, source_target_pairs={{0,1},{1,0},{2,3},{3,2},{4,5},{5,4},{6,7},{7,6},{8,9},{9,8},{10,11... | collective-permute-start | bytes 3145736 | tf_op jit(solution)/shard_map/ppermute | solution.py:49
  665.6 5.8 copy-start.10
  665.6 5.8 copy-start.14
  665.6 5.8 copy-start.16
  665.6 6.0 copy-start.35
  675.1 35.0 %collective-permute-start.34 = (bf16[23,1024]{1,0:T(8,128)(2,1)S(1)}, bf16[23,1024]{1,0:T(8,128)(2,1)S(1)}, u32[]{:S(2)}, u32[]{:S(2)}) collective-permute-start(bf16[23,1024]{1,0:T(8,128)(2,1)S(1)} %get-tuple-element.55), channel_id=1, source_target_pairs={{2,0},{4,2},{6,4},{8,6},{10,8},{12,10},{14,12},{16,14},{18,16},{20... | collective-permute-start | bytes 141320 | tf_op jit(solution)/shard_map/ppermute | solution.py:26
  677.1 33.1 %collective-permute-start.33 = (bf16[23,1024]{1,0:T(8,128)(2,1)S(1)}, bf16[23,1024]{1,0:T(8,128)(2,1)S(1)}, u32[]{:S(2)}, u32[]{:S(2)}) collective-permute-start(bf16[23,1024]{1,0:T(8,128)(2,1)S(1)} %get-tuple-element.54), channel_id=1, source_target_pairs={{0,2},{2,4},{4,6},{6,8},{8,10},{10,12},{12,14},{14,16},{16,18},{18... | collective-permute-start | bytes 141320 | tf_op jit(solution)/shard_map/ppermute | solution.py:25
  709.5 29.7 %collective-permute-start.1 = (bf16[2048,512]{0,1:T(8,128)(2,1)S(1)}, bf16[2048,512]{0,1:T(8,128)(2,1)}, u32[]{:S(2)}, u32[]{:S(2)}) collective-permute-start(bf16[2048,512]{0,1:T(8,128)(2,1)S(1)} %bitcast.53), channel_id=1, source_target_pairs={{0,1},{1,0},{2,3},{3,2},{4,5},{5,4},{6,7},{7,6},{8,9},{9,8},{10,11... | collective-permute-start | bytes 6291464 | tf_op jit(solution)/shard_map/ppermute | solution.py:49
  712.2 13.0 %copy-start.31 = (bf16[302,512]{0,1:T(8,128)(2,1)S(1)}, bf16[302,512]{0,1:T(8,128)(2,1)}, u32[]{:S(2)}) copy-start(bf16[302,512]{0,1:T(8,128)(2,1)} %copy.27) | copy-start | bytes 927748
  725.2 9.1 %copy-start.18 = (bf16[512,1024]{1,0:T(8,128)(2,1)S(1)}, bf16[512,1024]{1,0:T(8,128)(2,1)}, u32[]{:S(2)}) copy-start(bf16[512,1024]{1,0:T(8,128)(2,1)} %param.27) | copy-start | bytes 3145732
  725.2 9.7 %copy-start.19 = (bf16[512,1024]{1,0:T(8,128)(2,1)S(1)}, bf16[512,1024]{1,0:T(8,128)(2,1)}, u32[]{:S(2)}) copy-start(bf16[512,1024]{1,0:T(8,128)(2,1)} %param.26) | copy-start | bytes 3145732
  734.2 9.2 %collective-permute-start.35 = (bf16[2048,512]{0,1:T(8,128)(2,1)S(1)}, bf16[2048,512]{0,1:T(8,128)(2,1)S(1)}, u32[]{:S(2)}, u32[]{:S(2)}) collective-permute-start(bf16[2048,512]{0,1:T(8,128)(2,1)S(1)} %bitcast.58), channel_id=1, source_target_pairs={{0,1},{1,0},{2,3},{3,2},{4,5},{5,4},{6,7},{7,6},{8,9},{9,8},{10,11... | collective-permute-start | bytes 6291464 | tf_op jit(solution)/shard_map/ppermute | solution.py:49
  734.3 4.8 collective-permute-start.2
  734.9 8.5 %collective-permute-start.36 = (bf16[512,512]{1,0:T(8,128)(2,1)S(1)}, bf16[512,512]{1,0:T(8,128)(2,1)S(1)}, u32[]{:S(2)}, u32[]{:S(2)}) collective-permute-start(bf16[512,512]{1,0:T(8,128)(2,1)S(1)} %constant_dynamic-slice_fusion.37), channel_id=1, source_target_pairs={{0,1},{1,0},{2,3},{3,2},{4,5},{5,4},{6,7},{7,6},{8,9},{9,8},{10,11... | collective-permute-start | bytes 1572872 | tf_op jit(solution)/shard_map/ppermute | solution.py:49
  (14 other events, 45.6 us)

commit v2 on v0

--- a/solution.py
+++ b/solution.py
@@ -3,12 +3,15 @@
 import jax
 import jax.numpy as jnp
 from jax import lax
+from jax.experimental import pallas as pl
+from jax.experimental.pallas import tpu as pltpu
 from jax.sharding import PartitionSpec as P
 
 HD = 64
 PWIN = 8
 WINDOW = 512
 HALO = 23
+GROUP = 4
 
 
 EPS = 1e-05
@@ -27,6 +30,27 @@
     return value
 
 
+def along_far(value, by):
+    if by == 0:
+        return value
+    count = lax.axis_size("seq")
+    plane = count // GROUP
+    pairs = [(i, ((i // plane) ^ by) * plane + i % plane) for i in range(count)]
+    return lax.ppermute(value, "seq", pairs)
+
+
+def along_near(value, by):
+    if by == 0:
+        return value
+    return lax.ppermute(value, "seq", [(i, i ^ by) for i in range(lax.axis_size("seq"))])
+
+
+def along_ffn(value, by):
+    if by == 0:
+        return value
+    return lax.ppermute(value, "ffn", [(i, i ^ by) for i in range(lax.axis_size("ffn"))])
+
+
 def shifted(value, axis, by):
     count = lax.axis_size(axis)
     pairs = [(i, i + by) for i in range(count) if 0 <= i + by < count]
@@ -43,6 +67,45 @@
     row_max = jnp.max(masked, axis=-1, keepdims=True)
     exp_terms = jnp.exp(masked - row_max)
     return exp_terms / jnp.sum(exp_terms, axis=-1, keepdims=True)
+
+
+def cross_kernel(query_ref, key_ref, value_ref, bounds_ref, out_ref):
+    keys, count = key_ref.shape[0], query_ref.shape[1]
+    slot = lax.broadcasted_iota(jnp.int32, (keys, count), 0)
+    inside = (slot >= bounds_ref[0:1, :]) & (slot <= bounds_ref[1:2, :])
+    bias = jnp.where(inside, 0.0, -jnp.inf)
+    for head in range(query_ref.shape[0] // HD):
+        part = slice(head * HD, (head + 1) * HD)
+        scores = bias + jnp.dot(
+            key_ref[:, part], query_ref[part, :], preferred_element_type=jnp.float32
+        )
+        terms = jnp.exp(scores - jnp.max(scores, axis=0, keepdims=True))
+        weights = terms * (1.0 / jnp.sum(terms, axis=0, keepdims=True))
+        out_ref[part, :] = jnp.dot(
+            value_ref[part, :], weights.astype(jnp.bfloat16), preferred_element_type=jnp.float32
+        ).astype(jnp.bfloat16)
+
+
+def cross_attention(query, extended, first_slot, last_slot):
+    columns, count = query.shape
+    extended = jnp.pad(extended, ((0, -extended.shape[0] % 16), (0, 0)))
+    keys = extended.shape[0]
+    values = extended[:, columns:].T
+    bounds = jnp.stack([first_slot, last_slot] + [last_slot] * 6)
+    run = min(count, 512)
+    return pl.pallas_call(
+        cross_kernel,
+        grid=(count // run,),
+        in_specs=[
+            pl.BlockSpec((columns, run), lambda i: (0, i)),
+            pl.BlockSpec((keys, columns), lambda i: (0, 0)),
+            pl.BlockSpec((columns, keys), lambda i: (0, 0)),
+            pl.BlockSpec((8, run), lambda i: (0, i)),
+        ],
+        out_specs=pl.BlockSpec((columns, run), lambda i: (0, i)),
+        out_shape=jax.ShapeDtypeStruct((columns, count), jnp.bfloat16),
+        compiler_params=pltpu.CompilerParams(vmem_limit_bytes=32 * 1024 * 1024),
+    )(query, extended[:, :columns], values, bounds)
 
 
 def local(
@@ -61,46 +124,35 @@
     cross_out,
     self_out,
 ):
-    patch_count = patches.shape[0]
-    normed = row_normalize(patches).astype(jnp.bfloat16)
-
-    def add_rows(piece_rows):
-        return jnp.dot(normed, piece_rows, preferred_element_type=jnp.float32)
-
-    gate_sum = add_rows(lax.all_gather(gate_weight, "seq", axis=0, tiled=True))
-    up_sum = add_rows(lax.all_gather(up_weight, "seq", axis=0, tiled=True))
-    hidden = (jax.nn.silu(gate_sum) * up_sum).astype(jnp.bfloat16)
-    ffn_out = lax.dot_general(
-        hidden,
-        lax.all_gather(down_weight, "seq", axis=0, tiled=True),
-        (((1,), (1,)), ((), ())),
-        preferred_element_type=jnp.float32,
-    )
-    ffn_whole = lax.psum(ffn_out, "ffn")
-    global_out = (patches.astype(jnp.float32) + ffn_whole).astype(jnp.bfloat16)
+    patch_count, width = patches.shape
+    rows, units = gate_weight.shape
+    ring = lax.axis_size("seq")
+    plane = ring // GROUP
+    cores = lax.axis_size("ffn")
+    seq_at = lax.axis_index("seq")
+    core_at = lax.axis_index("ffn")
+    far, near = seq_at // plane, seq_at % plane
+
     head_cols = key_weight.shape[1]
     head_count = head_cols // HD
     score_scale = 1.0 / math.sqrt(HD)
     seq_index = lax.axis_index("seq")
-    keys_c = jnp.dot(global_out, key_weight, preferred_element_type=jnp.float32).astype(
-        jnp.bfloat16
-    )
-    values_c = jnp.dot(global_out, value_weight, preferred_element_type=jnp.float32).astype(
-        jnp.bfloat16
-    )
-    both_c = jnp.concatenate([keys_c, values_c], axis=1)
-    extended = padded(both_c, (("seq", 0),), HALO)
-    key_count = extended.shape[0]
-    key_index = seq_index * patch_count - HALO + jnp.arange(key_count, dtype=jnp.int32)
-    cross_mask = (
-        (key_index[None, :] <= byte_patch[:, None])
-        & (key_index[None, :] > byte_patch[:, None] - PWIN)
-        & (key_index[None, :] >= 0)
-    )
+
     byte_count = byte_states.shape[0]
-    query_c = jnp.dot(byte_states, cross_query, preferred_element_type=jnp.float32).astype(
-        jnp.bfloat16
-    )
+    out_cols = cross_out.shape[1] // cores
+
+    def out_share(context, weight, depth_axis):
+        total = 0.0
+        for k in range(cores):
+            block = lax.dynamic_slice_in_dim(weight, (core_at ^ k) * out_cols, out_cols, axis=1)
+            total += lax.dot_general(
+                along_ffn(context, k),
+                along_ffn(block, k),
+                (((depth_axis,), (0,)), ((), ())),
+                preferred_element_type=jnp.float32,
+            )
+        return total
+
     query_s = jnp.dot(byte_states, self_query, preferred_element_type=jnp.float32).astype(
         jnp.bfloat16
     )
@@ -108,18 +160,12 @@
     values_s = jnp.dot(byte_states, self_value, preferred_element_type=jnp.float32).astype(
         jnp.bfloat16
     )
-    query_here = query_c.reshape(byte_count, head_count, HD)
-    keys_here = extended[:, :head_cols].reshape(key_count, head_count, HD)
-    values_here = extended[:, head_cols:].reshape(key_count, head_count, HD)
-    cross_scores = (
-        jnp.einsum("qhd,khd->hqk", query_here, keys_here, preferred_element_type=jnp.float32)
+    query_c = (
+        lax.dot_general(
+            cross_query, byte_states, (((0,), (1,)), ((), ())), preferred_element_type=jnp.float32
+        )
         * score_scale
-    )
-    weights_c = masked_softmax(cross_scores, cross_mask[None]).astype(jnp.bfloat16)
-    context_c = jnp.einsum(
-        "hqk,khd->qhd", weights_c, values_here, preferred_element_type=jnp.float32
-    )
-    context_c = context_c.astype(jnp.bfloat16).reshape(byte_count, head_cols)
+    ).astype(jnp.bfloat16)
     both_s = jnp.concatenate([keys_s, values_s], axis=1)
     tail_rows = both_s[byte_count - WINDOW :]
     before = shifted(tail_rows, "seq", 1)
@@ -153,12 +199,120 @@
         "bhqk,bkhd->bqhd", weights_s, window_values, preferred_element_type=jnp.float32
     )
     context_s = context_s.astype(jnp.bfloat16).reshape(byte_count, head_cols)
-    partial_sum = jnp.dot(context_c, cross_out, preferred_element_type=jnp.float32) + jnp.dot(
-        context_s, self_out, preferred_element_type=jnp.float32
-    )
-    return lax.psum_scatter(partial_sum, "ffn", scatter_dimension=1, tiled=True).astype(
+
+    quarter = units // GROUP
+    head = min(quarter, -(-quarter // 256) * 128)
+    pieces = [(0, head), (head, quarter - head)]
+
+    def fetch_column(gate, up, at, size):
+        column = []
+        for k in range(GROUP):
+            start = (far ^ k) * quarter + at
+            both = jnp.concatenate(
+                [
+                    lax.dynamic_slice_in_dim(gate, start, size, axis=1),
+                    lax.dynamic_slice_in_dim(up, start, size, axis=1),
+                ],
+                axis=1,
+            )
+            column.append(along_far(both, k))
+        return jnp.concatenate(column, axis=0)
+
+    columns = [fetch_column(gate_weight, up_weight, *pieces[0])]
+    columns[0], patches, gate_weight, up_weight = lax.optimization_barrier(
+        (columns[0], patches, gate_weight, up_weight)
+    )
+    columns.append(fetch_column(gate_weight, up_weight, *pieces[1]))
+    down_blocks = [along_near(down_weight, j) for j in range(plane - 1)]
+
+    share = width // cores
+    mine = lax.dynamic_slice_in_dim(patches, core_at * share, share, axis=1)
+    held = jnp.zeros((GROUP * patch_count, share), patches.dtype)
+    for k in range(GROUP):
+        held = lax.dynamic_update_slice_in_dim(
+            held, along_far(mine, k), (far ^ k) * patch_count, axis=0
+        )
+    group = jnp.zeros((GROUP * patch_count, width), patches.dtype)
+    for k in range(cores):
+        group = lax.dynamic_update_slice_in_dim(
+            group, along_ffn(held, k), (core_at ^ k) * share, axis=1
+        )
+    normed = row_normalize(group).astype(jnp.bfloat16)
+    slabs = []
+    for j in range(plane):
+        picked = [
+            lax.dynamic_slice_in_dim(normed, ((far ^ k) * plane + (near ^ j)) * rows, rows, axis=1)
+            for k in range(GROUP)
+        ]
+        slabs.append(jnp.concatenate(picked, axis=1))
+
+    slabs, context_s = lax.optimization_barrier((slabs, context_s))
+    gathered = [[along_near(column, j) for j in range(plane)] for column in columns]
+    gathered[1], down_weight = lax.optimization_barrier((gathered[1], down_weight))
+    down_blocks.append(along_near(down_weight, plane - 1))
+
+    hidden_all = jnp.zeros((GROUP * patch_count, units), jnp.bfloat16)
+    for (at, size), blocks_here in zip(pieces, gathered):
+        sums = 0.0
+        for j in range(plane):
+            sums += jnp.dot(slabs[j], blocks_here[j], preferred_element_type=jnp.float32)
+        hidden = (jax.nn.silu(sums[:, :size]) * sums[:, size:]).astype(jnp.bfloat16)
+        for k in range(GROUP):
+            hidden_all = lax.dynamic_update_slice_in_dim(
+                hidden_all, along_far(hidden, k), (far ^ k) * quarter + at, axis=1
+            )
+
+    total_s = out_share(context_s, self_out, 1)
+    hidden_all, total_s, query_c = lax.optimization_barrier((hidden_all, total_s, query_c))
+    down = jnp.zeros((plane * rows, units), down_weight.dtype)
+    for j in range(plane):
+        down = lax.dynamic_update_slice_in_dim(
+            down, down_blocks[j], (near ^ j) * rows, axis=0
+        )
+    ffn_out = lax.dot_general(
+        hidden_all, down, (((1,), (1,)), ((), ())), preferred_element_type=jnp.float32
+    )
+    cut = plane * rows // cores
+    ffn_whole = 0.0
+    for k in range(cores):
+        ffn_whole += along_ffn(
+            lax.dynamic_slice_in_dim(ffn_out, (core_at ^ k) * cut, cut, axis=1), k
+        )
+    group_cut = lax.dynamic_slice_in_dim(group, (far * cores + core_at) * cut, cut, axis=1)
+    out_cut = (group_cut.astype(jnp.float32) + ffn_whole).astype(jnp.bfloat16)
+    returned = jnp.concatenate(
+        [
+            along_far(
+                lax.dynamic_slice_in_dim(out_cut, (far ^ k) * patch_count, patch_count, axis=0), k
+            )
+            for k in range(GROUP)
+        ],
+        axis=1,
+    )
+    global_out = jnp.zeros((patch_count, width), jnp.bfloat16)
+    for c in range(cores):
+        other = along_ffn(returned, c)
+        for k in range(GROUP):
+            global_out = lax.dynamic_update_slice_in_dim(
+                global_out,
+                other[:, k * cut : (k + 1) * cut],
+                ((far ^ k) * cores + (core_at ^ c)) * cut,
+                axis=1,
+            )
+    keys_c = jnp.dot(global_out, key_weight, preferred_element_type=jnp.float32).astype(
         jnp.bfloat16
     )
+    values_c = jnp.dot(global_out, value_weight, preferred_element_type=jnp.float32).astype(
+        jnp.bfloat16
+    )
+    both_c = jnp.concatenate([keys_c, values_c], axis=1)
+    extended = padded(both_c, (("seq", 0),), HALO)
+    first_key = seq_index * patch_count - HALO
+    last_slot = byte_patch - first_key
+    first_slot = jnp.maximum(last_slot - (PWIN - 1), -first_key)
+    context_c = cross_attention(query_c, extended, first_slot, last_slot)
+    total = total_s + out_share(context_c, cross_out, 0)
+    return total.astype(jnp.bfloat16)
 
 
 def solution(mesh):

time: 1140 us -> 708 us (0.62)
  waiting for transfers between devices: 875 us -> 299 us
  local copies, waits for them, and re-layouts: 45.9 us -> 126 us
  starting transfers between devices: 8.7 us -> 72.2 us
  matrix products: 157 us -> 126 us
  other arithmetic: 31.7 us -> 60.1 us
  Pallas kernels: 0 us -> 13.8 us
  between operations: 13.8 us -> 0.88 us
    all_gather x3 -> x0, waiting for transfers between devices: 814 us -> none  [the longest x1 312 us: local(): lax.all_gather(down_weight, 'seq', axis=0, tiled=True)]
    ppermute x0 -> x34, waiting for transfers between devices: none -> 288 us  [the longest x18 166 us: along_far(): return lax.ppermute(value, 'seq', pairs)]
    ppermute x0 -> x34, starting transfers between devices: none -> 62.7 us  [the longest x18 38.1 us: along_far(): return lax.ppermute(value, 'seq', pairs)]
    ppermute x1, waiting for transfers between devices: 39.8 us -> 0.01 us  [shifted(): return lax.ppermute(value, axis, pairs)]
    dynamic_update_slice x0 -> x23, local copies, waits for them, and re-layouts: none -> 38.3 us  [the longest x4 11.5 us: local(): lax.dynamic_update_slice_in_dim(down, down_blocks[j], (near ^ j) * rows,...]
    reduce_scatter x1 -> x0, waiting for transfers between devices: 18.9 us -> none  [local(): lax.psum_scatter(partial_sum, 'ffn', scatter_dimension=1, tiled=True)]
    dot_general x6 -> x14, matrix products: 66.6 us -> 50.8 us  [the longest x8 30.8 us: local(): jnp.dot(slabs[j], blocks_here[j], preferred_element_type=jnp.float32)]
    sub x2 -> x1, matrix products: 46.2 us -> 31 us  [masked_softmax(): exp_terms = jnp.exp(masked - row_max)]
  transfers between devices with their start and end apart: 8 -> 37, of which waited for: 5 -> 18; matrix products, arithmetic and copies ran while one was open for 14% -> 37% of each run, Pallas kernels for 0% -> 0%
where the time goes in v2:
time: 708 us; the launch traced here: 698 us
  waiting for transfers between devices  299 us (42%)
  local copies, waits for them, and re-layouts  126 us (18%)
  matrix products  126 us (18%)
  starting transfers between devices  72.2 us (10%)
  other arithmetic  60.1 us (8%)
  Pallas kernels  13.8 us (2%)
    ppermute x18, waiting for transfers between devices, along_far(): return lax.ppermute(value, 'seq', pairs)  166 us
    ppermute x9, waiting for transfers between devices, along_near(): lax.ppermute(value, 'seq', [(i, i ^ by) for i in range(lax.axis_size('seq...  115 us
    ppermute x18, starting transfers between devices, along_far(): return lax.ppermute(value, 'seq', pairs)  38.1 us
    sub x1, matrix products, masked_softmax(): exp_terms = jnp.exp(masked - row_max)  31 us
    dot_general x8, matrix products, local(): jnp.dot(slabs[j], blocks_here[j], preferred_element_type=jnp.float32)  30.8 us
    dot_general x1, matrix products, local(): jnp.einsum('bhqk,bkhd->bqhd', weights_s, window_values, preferred_element...  26.5 us
    concatenate x2, other arithmetic, local(): both_s = jnp.concatenate([keys_s, values_s], axis=1)  22.9 us
    ppermute x7, starting transfers between devices, along_ffn(): lax.ppermute(value, 'ffn', [(i, i ^ by) for i in range(lax.axis_size('ffn...  19.3 us
  transfers between devices with their start and end apart: 37, of which 18 were waited for; matrix products, arithmetic and copies ran while one was open for 37% of the time, Pallas kernels for 0%

profile of v2, /device:TPU:23, one launch (start us, length us, event | category | flops | bytes accessed | tf_op | source)
XLA Modules:
  0.0 698.3 jit_solution(17222390132389355885)
XLA Ops:
  14.6 4.3 collective-permute-start.7
  20.1 6.3 convolution_convert_fusion
  28.8 3.4 broadcast.86.clone.1
  32.2 2.9 constant_dynamic-update-slice_fusion.7
  35.2 6.2 reshape.102
  41.5 3.3 broadcast_and_fusion
  44.8 7.3 %collective-permute-done.2 = bf16[256,1024]{1,0:T(8,128)(2,1)} collective-permute-done((bf16[256,1024]{1,0:T(8,128)(2,1)}, bf16[256,1024]{1,0:T(8,128)(2,1)}, u32[]{:S(2)}, u32[]{:S(2)}) %collective-permute-start.2) | collective-permute-done | bytes 524320 | tf_op jit(solution)/shard_map/ppermute | solution.py:39
  52.1 2.9 pad_maximum_fusion.3
  63.6 4.1 copy.22
  71.9 6.1 collective-permute-done.15
  78.0 23.2 %collective-permute-start.3 = (bf16[256,2048]{0,1:T(8,128)(2,1)}, bf16[256,2048]{0,1:T(8,128)(2,1)}, u32[]{:S(2)}, u32[]{:S(2)}) collective-permute-start(bf16[256,2048]{0,1:T(8,128)(2,1)} %get-tuple-element.48), channel_id=1, source_target_pairs={{0,8},{2,10},{4,12},{6,14},{8,0},{10,2},{12,4},{14,6},{16,24},{18,... | collective-permute-start | bytes 3145736 | tf_op jit(solution)/shard_map/ppermute | solution.py:39
  101.1 7.2 %collective-permute-done.16 = bf16[256,768]{1,0:T(8,128)(2,1)} collective-permute-done((bf16[256,768]{1,0:T(8,128)(2,1)}, bf16[256,768]{1,0:T(8,128)(2,1)}, u32[]{:S(2)}, u32[]{:S(2)}) %collective-permute-start.16) | collective-permute-done | bytes 393248 | tf_op jit(solution)/shard_map/ppermute | solution.py:39
  110.9 21.6 %pad_maximum_fusion = (bf16[2048,1024]{0,1:T(8,128)(2,1)}, bf16[2048,1024]{0,1:T(8,128)(2,1)}) fusion(bf16[2048,512]{0,1:T(8,128)(2,1)S(1)} %copy-done.6, bf16[2048,512]{0,1:T(8,128)(2,1)S(1)} %copy-done.8, bf16[512,1024]{0,1:T(8,128)(2,1)} %collective-permute-done.7), kind=kLoop, calls=%fused_computation.15 | loop fusion | flops 20971520 | bytes 13631488 | tf_op jit(solution)/shard_map/concatenate | solution.py:169
  132.5 7.9 %reshape.96 = bf16[4,512,1024]{1,0,2:T(4,128)(2,1)} reshape(bf16[2048,1024]{0,1:T(8,128)(2,1)} %get-tuple-element.68) | data formatting | bytes 8388608 | tf_op jit(solution)/shard_map/reshape | solution.py:174
  140.4 5.7 constant_dynamic-update-slice_fusion.23
  146.1 7.9 %reshape.97 = bf16[4,512,1024]{1,0,2:T(4,128)(2,1)} reshape(bf16[2048,1024]{0,1:T(8,128)(2,1)} %get-tuple-element.67) | data formatting | bytes 8388608 | tf_op jit(solution)/shard_map/reshape | solution.py:175
  154.1 5.7 constant_dynamic-update-slice_fusion.22
  159.8 7.0 %fusion.39 = (bf16[4,1024,512]{1,0,2:T(4,128)(2,1)S(1)}, bf16[4,1024,512]{1,0,2:T(4,128)(2,1)}) fusion(bf16[4,1024,1024]{1,0,2:T(4,128)(2,1)} %constant_dynamic-update-slice_fusion.22), kind=kLoop, calls=%fused_computation.151 | loop fusion | bytes 16777216 | tf_op jit(solution)/shard_map/slice | solution.py:177
  166.8 3.4 copy.25
  170.1 31.0 %fusion.40 = (f32[4,8,512]{2,1,0:T(8,128)S(1)}, f32[4,8,512,1024]{3,2,1,0:T(8,128)}) fusion(pred[4,512,1024]{2,1,0:T(8,128)(4,1)} %broadcast_and_fusion, bf16[4,1024,8,64]{1,3,2,0:T(8,128)(2,1)} %bitcast.60, bf16[4,512,8,64]{3,2,1,0:T(8,128)(2,1)} %reshape.102), kind=kOutput, calls=%fused_computation.152 | convolution fusion | flops 2214593536 | bytes 75563008 | tf_op jit(solution)/shard_map/sub | solution.py:68
  201.1 5.5 copy.23
  211.4 2.6 collective-permute-start.19
  216.4 3.2 collective-permute-start.6
  219.6 26.5 %convert_bitcast_fusion = bf16[4,512,8,64]{1,3,2,0:T(8,128)(2,1)} fusion(bf16[4,1024,8,64]{1,3,2,0:T(8,128)(2,1)} %bitcast.59, f32[4,8,512,1024]{3,2,1,0:T(8,128)} %get-tuple-element.95, f32[4,8,512]{2,1,0:T(8,128)S(1)} %get-tuple-element.94), kind=kOutput, calls=%fused_computation.39 | convolution fusion | flops 2182086656 | bytes 73465856 | tf_op jit(solution)/shard_map/bhqk,bkhd->bqhd/dot_general | solution.py:198
  246.1 3.2 copy.27
  251.0 2.7 constant_dynamic-update-slice_fusion.17
  253.7 2.9 constant_dynamic-update-slice_fusion.6
  256.6 2.9 constant_dynamic-update-slice_fusion.5
  259.5 17.1 %collective-permute-done.18 = bf16[1024,768]{1,0:T(8,128)(2,1)} collective-permute-done((bf16[1024,768]{1,0:T(8,128)(2,1)}, bf16[1024,768]{1,0:T(8,128)(2,1)}, u32[]{:S(2)}, u32[]{:S(2)}) %collective-permute-start.18) | collective-permute-done | bytes 1572896 | tf_op jit(solution)/shard_map/ppermute | solution.py:45
  279.0 2.7 constant_dynamic-update-slice_fusion.16
  285.0 9.2 %fusion.9 = bf16[1024,4096]{0,1:T(8,128)(2,1)} fusion(bf16[1024,4096]{0,1:T(8,128)(2,1)} %copy-done.3, f32[1024]{0:T(1024)S(1)} %add_rsqrt_fusion), kind=kLoop, calls=%fused_computation.13 | loop fusion | flops 12582912 | bytes 16781312 | tf_op jit(solution)/shard_map/convert_element_type | solution.py:240
  294.2 4.4 constant_dynamic-slice_fusion.18
  299.4 5.0 fusion.45
  304.4 14.8 %collective-permute-done.8 = bf16[1024,1024]{1,0:T(8,128)(2,1)} collective-permute-done((bf16[1024,1024]{1,0:T(8,128)(2,1)}, bf16[1024,1024]{1,0:T(8,128)(2,1)}, u32[]{:S(2)}, u32[]{:S(2)}) %collective-permute-start.8) | collective-permute-done | bytes 2097184 | tf_op jit(solution)/shard_map/ppermute | solution.py:45
  319.2 4.0 fusion.46
  323.2 82.6 %collective-permute-done.9 = bf16[1024,1024]{1,0:T(8,128)(2,1)} collective-permute-done((bf16[1024,1024]{1,0:T(8,128)(2,1)}, bf16[1024,1024]{1,0:T(8,128)(2,1)}, u32[]{:S(2)}, u32[]{:S(2)}) %collective-permute-start.9) | collective-permute-done | bytes 2097184 | tf_op jit(solution)/shard_map/ppermute | solution.py:45
  405.8 4.0 fusion.47
  409.8 4.5 add_add_fusion
  415.5 3.0 collective-permute-start.11
  419.7 4.4 collective-permute-start.23
  424.2 3.3 fusion.49
  427.4 3.5 fusion.48
  430.9 3.3 fusion.50
  434.2 3.4 add_add_fusion.1
  437.7 22.1 %collective-permute-done.11 = bf16[1024,512]{1,0:T(8,128)(2,1)} collective-permute-done((bf16[1024,512]{1,0:T(8,128)(2,1)S(1)}, bf16[1024,512]{1,0:T(8,128)(2,1)}, u32[]{:S(2)}, u32[]{:S(2)}) %collective-permute-start.11) | collective-permute-done | bytes 1048608 | tf_op jit(solution)/shard_map/ppermute | solution.py:39
  459.8 3.0 collective-permute-start.24
  464.3 42.2 %collective-permute-done.13 = bf16[1024,512]{1,0:T(8,128)(2,1)S(1)} collective-permute-done((bf16[1024,512]{1,0:T(8,128)(2,1)S(1)}, bf16[1024,512]{1,0:T(8,128)(2,1)S(1)}, u32[]{:S(2)}, u32[]{:S(2)}) %collective-permute-start.13) | collective-permute-done | bytes 1048608 | tf_op jit(solution)/shard_map/ppermute | solution.py:39
  509.9 2.9 constant_dynamic-update-slice_fusion.4
  514.1 21.5 %collective-permute-done.20 = bf16[1024,384]{1,0:T(8,128)(2,1)S(1)} collective-permute-done((bf16[1024,384]{1,0:T(8,128)(2,1)S(1)}, bf16[1024,384]{1,0:T(8,128)(2,1)S(1)}, u32[]{:S(2)}, u32[]{:S(2)}) %collective-permute-start.20) | collective-permute-done | bytes 786464 | tf_op jit(solution)/shard_map/ppermute | solution.py:39
  538.5 34.6 %collective-permute-done.22 = bf16[1024,384]{1,0:T(8,128)(2,1)S(1)} collective-permute-done((bf16[1024,384]{1,0:T(8,128)(2,1)S(1)}, bf16[1024,384]{1,0:T(8,128)(2,1)S(1)}, u32[]{:S(2)}, u32[]{:S(2)}) %collective-permute-start.22) | collective-permute-done | bytes 786464 | tf_op jit(solution)/shard_map/ppermute | solution.py:39
  573.3 3.5 convolution_add_fusion
  576.7 10.3 %fusion.51 = f32[1024,1024]{0,1:T(8,128)S(1)} fusion(bf16[1024,3584]{1,0:T(8,128)(2,1)S(1)} %constant_dynamic-update-slice_fusion.8, bf16[1024,3584]{1,0:T(8,128)(2,1)} %constant_dynamic-update-slice_fusion.4), kind=kOutput, calls=%fused_computation.159 | convolution fusion | flops 7516192768 | bytes 18874368 | tf_op jit(solution)/shard_map/dot_general | solution.py:272
  590.4 5.9 collective-permute-start.28
  596.3 4.1 collective-permute-done.28
  600.4 3.1 add_convert_fusion.1
  607.8 7.4 %collective-permute-done.29 = bf16[256,512]{0,1:T(8,128)(2,1)S(1)} collective-permute-done((bf16[256,512]{0,1:T(8,128)(2,1)S(1)}, bf16[256,512]{0,1:T(8,128)(2,1)S(1)}, u32[]{:S(2)}, u32[]{:S(2)}) %collective-permute-start.29) | collective-permute-done | bytes 262176 | tf_op jit(solution)/shard_map/ppermute | solution.py:39
  615.2 3.1 collective-permute-done.30
  618.3 12.2 %collective-permute-done.31 = bf16[256,512]{0,1:T(8,128)(2,1)S(1)} collective-permute-done((bf16[256,512]{0,1:T(8,128)(2,1)S(1)}, bf16[256,512]{0,1:T(8,128)(2,1)S(1)}, u32[]{:S(2)}, u32[]{:S(2)}) %collective-permute-start.31) | collective-permute-done | bytes 262176 | tf_op jit(solution)/shard_map/ppermute | solution.py:39
  643.8 4.7 convolution_convert_fusion.3
  653.9 3.4 collective-permute-start.34
  658.0 4.0 collective-permute-done.33
  662.0 6.5 collective-permute-done.34
  674.7 13.8 %shard_map.136 = bf16[512,2048]{1,0:T(8,128)(2,1)S(1)} custom-call(bf16[512,2048]{1,0:T(8,128)(2,1)S(1)} %multiply_convert_fusion.query_ref, bf16[304,512]{1,0:T(8,128)(2,1)S(1)} %copy-done.1, bf16[512,304]{1,0:T(8,128)(2,1)S(1)} %get-tuple-element.90.value_ref, s32[8,2048]{1,0:T(8,128)S(1)} %copy-done.2), custom_call_target="tpu_custom_call" | custom-call | tf_op jit(solution)/shard_map/pallas_call | solution.py:96
  691.2 3.1 collective-permute-done.36
  (166 shorter events, 99.8 us)
Async XLA Ops:
  0.0 62.7 %copy-start = (bf16[512,1024]{1,0:T(8,128)(2,1)S(1)}, bf16[512,1024]{1,0:T(8,128)(2,1)}, u32[]{:S(2)}) copy-start(bf16[512,1024]{1,0:T(8,128)(2,1)} %param.27) | copy-start | bytes 3145732
  0.0 7.9 %copy-start.21 = (bf16[2048,1024]{1,0:T(8,128)(2,1)S(1)}, bf16[2048,1024]{1,0:T(8,128)(2,1)}, u32[]{:S(2)}) copy-start(bf16[2048,1024]{1,0:T(8,128)(2,1)} %param.20) | copy-start | bytes 12582916
  0.0 7.9 %copy-start.24 = (bf16[1024,512]{1,0:T(8,128)(2,1)S(1)}, bf16[1024,512]{1,0:T(8,128)(2,1)}, u32[]{:S(2)}) copy-start(bf16[1024,512]{1,0:T(8,128)(2,1)} %param.25) | copy-start | bytes 3145732
  3.4 41.4 %collective-permute-start = (bf16[256,1024]{1,0:T(8,128)(2,1)}, bf16[256,1024]{1,0:T(8,128)(2,1)}, u32[]{:S(2)}, u32[]{:S(2)}) collective-permute-start(bf16[256,1024]{1,0:T(8,128)(2,1)} %pad_maximum_fusion.10), channel_id=1, source_target_pairs={{0,8},{2,10},{4,12},{6,14},{8,0},{10,2},{12,4},{14,6},{16,24},{18,... | collective-permute-start | bytes 1572872 | tf_op jit(solution)/shard_map/ppermute | solution.py:39
  5.6 39.2 %collective-permute-start.1 = (bf16[256,1024]{1,0:T(8,128)(2,1)}, bf16[256,1024]{1,0:T(8,128)(2,1)}, u32[]{:S(2)}, u32[]{:S(2)}) collective-permute-start(bf16[256,1024]{1,0:T(8,128)(2,1)} %pad_maximum_fusion.11), channel_id=1, source_target_pairs={{0,16},{2,18},{4,20},{6,22},{8,24},{10,26},{12,28},{14,30},{16,0},... | collective-permute-start | bytes 1572872 | tf_op jit(solution)/shard_map/ppermute | solution.py:39
  6.6 3.8 copy-start.25
  6.6 45.6 %collective-permute-start.2 = (bf16[256,1024]{1,0:T(8,128)(2,1)}, bf16[256,1024]{1,0:T(8,128)(2,1)}, u32[]{:S(2)}, u32[]{:S(2)}) collective-permute-start(bf16[256,1024]{1,0:T(8,128)(2,1)} %pad_maximum_fusion.12), channel_id=1, source_target_pairs={{0,24},{2,26},{4,28},{6,30},{8,16},{10,18},{12,20},{14,22},{16,8},... | collective-permute-start | bytes 1572872 | tf_op jit(solution)/shard_map/ppermute | solution.py:39
  10.4 2.5 copy-start.5
  12.9 1.6 copy-start.7
  14.6 96.3 %collective-permute-start.7 = (bf16[512,1024]{0,1:T(8,128)(2,1)}, bf16[512,1024]{0,1:T(8,128)(2,1)}, u32[]{:S(2)}, u32[]{:S(2)}) collective-permute-start(bf16[512,1024]{0,1:T(8,128)(2,1)} %fusion.24), channel_id=1, source_target_pairs={{0,2},{2,4},{4,6},{6,8},{8,10},{10,12},{12,14},{14,16},{16,18},{18... | collective-permute-start | bytes 3145736 | tf_op jit(solution)/shard_map/ppermute | solution.py:57
  18.8 197.6 %collective-permute-start.25 = (bf16[256,3584]{1,0:T(8,128)(2,1)}, bf16[256,3584]{1,0:T(8,128)(2,1)}, u32[]{:S(2)}, u32[]{:S(2)}) collective-permute-start(bf16[256,3584]{1,0:T(8,128)(2,1)} %param.17), channel_id=1, source_target_pairs={{0,2},{2,0},{4,6},{6,4},{8,10},{10,8},{12,14},{14,12},{16,18},{18,... | collective-permute-start | bytes 5505032 | tf_op jit(solution)/shard_map/ppermute | solution.py:45
  20.1 6.3 copy-start.22
  20.1 6.3 copy-start.26
  58.5 13.2 %collective-permute-start.14 = (bf16[256,768]{1,0:T(8,128)(2,1)}, bf16[256,768]{1,0:T(8,128)(2,1)}, u32[]{:S(2)}, u32[]{:S(2)}) collective-permute-start(bf16[256,768]{1,0:T(8,128)(2,1)} %pad_maximum_fusion.13), channel_id=1, source_target_pairs={{0,8},{2,10},{4,12},{6,14},{8,0},{10,2},{12,4},{14,6},{16,24},{18,... | collective-permute-start | bytes 1179656 | tf_op jit(solution)/shard_map/ppermute | solution.py:39
  59.3 18.6 %collective-permute-start.15 = (bf16[256,768]{1,0:T(8,128)(2,1)}, bf16[256,768]{1,0:T(8,128)(2,1)}, u32[]{:S(2)}, u32[]{:S(2)}) collective-permute-start(bf16[256,768]{1,0:T(8,128)(2,1)} %pad_maximum_fusion.14), channel_id=1, source_target_pairs={{0,16},{2,18},{4,20},{6,22},{8,24},{10,26},{12,28},{14,30},{16,0},... | collective-permute-start | bytes 1179656 | tf_op jit(solution)/shard_map/ppermute | solution.py:39
  61.4 47.0 %collective-permute-start.16 = (bf16[256,768]{1,0:T(8,128)(2,1)}, bf16[256,768]{1,0:T(8,128)(2,1)}, u32[]{:S(2)}, u32[]{:S(2)}) collective-permute-start(bf16[256,768]{1,0:T(8,128)(2,1)} %pad_maximum_fusion.15), channel_id=1, source_target_pairs={{0,24},{2,26},{4,28},{6,30},{8,16},{10,18},{12,20},{14,22},{16,8},... | collective-permute-start | bytes 1179656 | tf_op jit(solution)/shard_map/ppermute | solution.py:39
  67.7 2.5 copy-start.9
  70.1 40.7 %copy-start.6 = (bf16[2048,512]{0,1:T(8,128)(2,1)S(1)}, bf16[2048,512]{0,1:T(8,128)(2,1)}, u32[]{:S(2)}) copy-start(bf16[2048,512]{0,1:T(8,128)(2,1)} %copy-done.5) | copy-start | bytes 6291460
  70.1 40.7 %copy-start.8 = (bf16[2048,512]{0,1:T(8,128)(2,1)S(1)}, bf16[2048,512]{0,1:T(8,128)(2,1)}, u32[]{:S(2)}) copy-start(bf16[2048,512]{0,1:T(8,128)(2,1)} %copy-done.7) | copy-start | bytes 6291460
  71.7 184.9 %collective-permute-start.26 = (bf16[256,3584]{1,0:T(8,128)(2,1)}, bf16[256,3584]{1,0:T(8,128)(2,1)}, u32[]{:S(2)}, u32[]{:S(2)}) collective-permute-start(bf16[256,3584]{1,0:T(8,128)(2,1)} %param.17), channel_id=1, source_target_pairs={{0,4},{2,6},{4,0},{6,2},{8,12},{10,14},{12,8},{14,10},{16,20},{18,... | collective-permute-start | bytes 5505032 | tf_op jit(solution)/shard_map/ppermute | solution.py:45
  78.0 128.7 %collective-permute-start.3 = (bf16[256,2048]{0,1:T(8,128)(2,1)}, bf16[256,2048]{0,1:T(8,128)(2,1)}, u32[]{:S(2)}, u32[]{:S(2)}) collective-permute-start(bf16[256,2048]{0,1:T(8,128)(2,1)} %get-tuple-element.48), channel_id=1, source_target_pairs={{0,8},{2,10},{4,12},{6,14},{8,0},{10,2},{12,4},{14,6},{16,24},{18,... | collective-permute-start | bytes 3145736 | tf_op jit(solution)/shard_map/ppermute | solution.py:39
  108.4 100.7 %collective-permute-start.4 = (bf16[256,2048]{0,1:T(8,128)(2,1)}, bf16[256,2048]{0,1:T(8,128)(2,1)}, u32[]{:S(2)}, u32[]{:S(2)}) collective-permute-start(bf16[256,2048]{0,1:T(8,128)(2,1)} %get-tuple-element.48), channel_id=1, source_target_pairs={{0,16},{2,18},{4,20},{6,22},{8,24},{10,26},{12,28},{14,30},{16,0},... | collective-permute-start | bytes 3145736 | tf_op jit(solution)/shard_map/ppermute | solution.py:39
  110.8 100.5 %collective-permute-start.5 = (bf16[256,2048]{0,1:T(8,128)(2,1)}, bf16[256,2048]{0,1:T(8,128)(2,1)}, u32[]{:S(2)}, u32[]{:S(2)}) collective-permute-start(bf16[256,2048]{0,1:T(8,128)(2,1)} %get-tuple-element.48), channel_id=1, source_target_pairs={{0,24},{2,26},{4,28},{6,30},{8,16},{10,18},{12,20},{14,22},{16,8},... | collective-permute-start | bytes 3145736 | tf_op jit(solution)/shard_map/ppermute | solution.py:39
  206.7 52.8 %collective-permute-start.17 = (bf16[1024,768]{1,0:T(8,128)(2,1)}, bf16[1024,768]{1,0:T(8,128)(2,1)}, u32[]{:S(2)}, u32[]{:S(2)}) collective-permute-start(bf16[1024,768]{1,0:T(8,128)(2,1)} %pad_maximum_fusion.8), channel_id=1, source_target_pairs={{0,2},{2,0},{4,6},{6,4},{8,10},{10,8},{12,14},{14,12},{16,18},{18,... | collective-permute-start | bytes 4718600 | tf_op jit(solution)/shard_map/ppermute | solution.py:45
  209.1 67.6 %collective-permute-start.18 = (bf16[1024,768]{1,0:T(8,128)(2,1)}, bf16[1024,768]{1,0:T(8,128)(2,1)}, u32[]{:S(2)}, u32[]{:S(2)}) collective-permute-start(bf16[1024,768]{1,0:T(8,128)(2,1)} %pad_maximum_fusion.8), channel_id=1, source_target_pairs={{0,4},{2,6},{4,0},{6,2},{8,12},{10,14},{12,8},{14,10},{16,20},{18,... | collective-permute-start | bytes 4718600 | tf_op jit(solution)/shard_map/ppermute | solution.py:45
  211.4 65.4 %collective-permute-start.19 = (bf16[1024,768]{1,0:T(8,128)(2,1)}, bf16[1024,768]{1,0:T(8,128)(2,1)}, u32[]{:S(2)}, u32[]{:S(2)}) collective-permute-start(bf16[1024,768]{1,0:T(8,128)(2,1)} %pad_maximum_fusion.8), channel_id=1, source_target_pairs={{0,6},{2,4},{4,2},{6,0},{8,14},{10,12},{12,10},{14,8},{16,22},{18,... | collective-permute-start | bytes 4718600 | tf_op jit(solution)/shard_map/ppermute | solution.py:45
  216.4 62.6 %collective-permute-start.6 = (bf16[1024,2048]{0,1:T(8,128)(2,1)}, bf16[1024,2048]{0,1:T(8,128)(2,1)}, u32[]{:S(2)}, u32[]{:S(2)}) collective-permute-start(bf16[1024,2048]{0,1:T(8,128)(2,1)} %constant_dynamic-update-slice_fusion.18), channel_id=1, source_target_pairs={{0,1},{1,0},{2,3},{3,2},{4,5},{5,4},{6,7},{7,6},{8,9},{9,8},{10,11... | collective-permute-start | bytes 12582920 | tf_op jit(solution)/shard_map/ppermute | solution.py:51
  256.6 62.6 %collective-permute-start.8 = (bf16[1024,1024]{1,0:T(8,128)(2,1)}, bf16[1024,1024]{1,0:T(8,128)(2,1)}, u32[]{:S(2)}, u32[]{:S(2)}) collective-permute-start(bf16[1024,1024]{1,0:T(8,128)(2,1)} %pad_maximum_fusion.3), channel_id=1, source_target_pairs={{0,2},{2,0},{4,6},{6,4},{8,10},{10,8},{12,14},{14,12},{16,18},{18,... | collective-permute-start | bytes 6291464 | tf_op jit(solution)/shard_map/ppermute | solution.py:45
  259.5 146.3 %collective-permute-start.9 = (bf16[1024,1024]{1,0:T(8,128)(2,1)}, bf16[1024,1024]{1,0:T(8,128)(2,1)}, u32[]{:S(2)}, u32[]{:S(2)}) collective-permute-start(bf16[1024,1024]{1,0:T(8,128)(2,1)} %pad_maximum_fusion.3), channel_id=1, source_target_pairs={{0,4},{2,6},{4,0},{6,2},{8,12},{10,14},{12,8},{14,10},{16,20},{18,... | collective-permute-start | bytes 6291464 | tf_op jit(solution)/shard_map/ppermute | solution.py:45
  276.6 133.2 %collective-permute-start.10 = (bf16[1024,1024]{1,0:T(8,128)(2,1)}, bf16[1024,1024]{1,0:T(8,128)(2,1)}, u32[]{:S(2)}, u32[]{:S(2)}) collective-permute-start(bf16[1024,1024]{1,0:T(8,128)(2,1)} %pad_maximum_fusion.3), channel_id=1, source_target_pairs={{0,6},{2,4},{4,2},{6,0},{8,14},{10,12},{12,10},{14,8},{16,22},{18,... | collective-permute-start | bytes 6291464 | tf_op jit(solution)/shard_map/ppermute | solution.py:45
  276.8 231.8 %collective-permute-start.27 = (bf16[256,3584]{1,0:T(8,128)(2,1)}, bf16[256,3584]{1,0:T(8,128)(2,1)}, u32[]{:S(2)}, u32[]{:S(2)}) collective-permute-start(bf16[256,3584]{1,0:T(8,128)(2,1)} %param.17), channel_id=1, source_target_pairs={{0,6},{2,4},{4,2},{6,0},{8,14},{10,12},{12,10},{14,8},{16,22},{18,... | collective-permute-start | bytes 5505032 | tf_op jit(solution)/shard_map/ppermute | solution.py:45
  281.7 3.3 copy-start.3
  299.4 5.0 copy-start.13
  415.5 11.9 %copy-start.14 = (bf16[1024,1024]{0,1:T(8,128)(2,1)S(1)}, bf16[1024,1024]{0,1:T(8,128)(2,1)}, u32[]{:S(2)}) copy-start(bf16[1024,1024]{0,1:T(8,128)(2,1)} %copy-done.13) | copy-start | bytes 6291460
  415.5 44.3 %collective-permute-start.11 = (bf16[1024,512]{1,0:T(8,128)(2,1)S(1)}, bf16[1024,512]{1,0:T(8,128)(2,1)}, u32[]{:S(2)}, u32[]{:S(2)}) collective-permute-start(bf16[1024,512]{1,0:T(8,128)(2,1)S(1)} %get-tuple-element.46), channel_id=1, source_target_pairs={{0,8},{2,10},{4,12},{6,14},{8,0},{10,2},{12,4},{14,6},{16,24},{18,... | collective-permute-start | bytes 3145736 | tf_op jit(solution)/shard_map/ppermute | solution.py:39
  418.5 45.7 %collective-permute-start.12 = (bf16[1024,512]{1,0:T(8,128)(2,1)S(1)}, bf16[1024,512]{1,0:T(8,128)(2,1)S(1)}, u32[]{:S(2)}, u32[]{:S(2)}) collective-permute-start(bf16[1024,512]{1,0:T(8,128)(2,1)S(1)} %get-tuple-element.46), channel_id=1, source_target_pairs={{0,16},{2,18},{4,20},{6,22},{8,24},{10,26},{12,28},{14,30},{16,0},... | collective-permute-start | bytes 3145736 | tf_op jit(solution)/shard_map/ppermute | solution.py:39
  418.5 88.1 %collective-permute-start.13 = (bf16[1024,512]{1,0:T(8,128)(2,1)S(1)}, bf16[1024,512]{1,0:T(8,128)(2,1)S(1)}, u32[]{:S(2)}, u32[]{:S(2)}) collective-permute-start(bf16[1024,512]{1,0:T(8,128)(2,1)S(1)} %get-tuple-element.46), channel_id=1, source_target_pairs={{0,24},{2,26},{4,28},{6,30},{8,16},{10,18},{12,20},{14,22},{16,8},... | collective-permute-start | bytes 3145736 | tf_op jit(solution)/shard_map/ppermute | solution.py:39
  419.7 153.5 %collective-permute-start.23 = (bf16[2048,512]{0,1:T(8,128)(2,1)S(1)}, bf16[2048,512]{0,1:T(8,128)(2,1)S(1)}, u32[]{:S(2)}, u32[]{:S(2)}) collective-permute-start(bf16[2048,512]{0,1:T(8,128)(2,1)S(1)} %bitcast.56), channel_id=1, source_target_pairs={{0,1},{1,0},{2,3},{3,2},{4,5},{5,4},{6,7},{7,6},{8,9},{9,8},{10,11... | collective-permute-start | bytes 6291464 | tf_op jit(solution)/shard_map/ppermute | solution.py:51
  434.2 25.6 %copy-start.19 = (bf16[512,512]{1,0:T(8,128)(2,1)S(1)}, bf16[512,512]{1,0:T(8,128)(2,1)}, u32[]{:S(2)}) copy-start(bf16[512,512]{1,0:T(8,128)(2,1)} %constant_dynamic-slice_fusion.6) | copy-start | bytes 1572868
  459.8 113.4 %collective-permute-start.24 = (bf16[512,512]{1,0:T(8,128)(2,1)S(1)}, bf16[512,512]{1,0:T(8,128)(2,1)S(1)}, u32[]{:S(2)}, u32[]{:S(2)}) collective-permute-start(bf16[512,512]{1,0:T(8,128)(2,1)S(1)} %copy-done.19), channel_id=1, source_target_pairs={{0,1},{1,0},{2,3},{3,2},{4,5},{5,4},{6,7},{7,6},{8,9},{9,8},{10,11... | collective-permute-start | bytes 1572872 | tf_op jit(solution)/shard_map/ppermute | solution.py:51
  507.2 28.4 %collective-permute-start.20 = (bf16[1024,384]{1,0:T(8,128)(2,1)S(1)}, bf16[1024,384]{1,0:T(8,128)(2,1)S(1)}, u32[]{:S(2)}, u32[]{:S(2)}) collective-permute-start(bf16[1024,384]{1,0:T(8,128)(2,1)S(1)} %get-tuple-element.44), channel_id=1, source_target_pairs={{0,8},{2,10},{4,12},{6,14},{8,0},{10,2},{12,4},{14,6},{16,24},{18,... | collective-permute-start | bytes 2359304 | tf_op jit(solution)/shard_map/ppermute | solution.py:39
  507.2 31.1 %collective-permute-start.21 = (bf16[1024,384]{1,0:T(8,128)(2,1)S(1)}, bf16[1024,384]{1,0:T(8,128)(2,1)S(1)}, u32[]{:S(2)}, u32[]{:S(2)}) collective-permute-start(bf16[1024,384]{1,0:T(8,128)(2,1)S(1)} %get-tuple-element.44), channel_id=1, source_target_pairs={{0,16},{2,18},{4,20},{6,22},{8,24},{10,26},{12,28},{14,30},{16,0},... | collective-permute-start | bytes 2359304 | tf_op jit(solution)/shard_map/ppermute | solution.py:39
  508.6 64.5 %collective-permute-start.22 = (bf16[1024,384]{1,0:T(8,128)(2,1)S(1)}, bf16[1024,384]{1,0:T(8,128)(2,1)S(1)}, u32[]{:S(2)}, u32[]{:S(2)}) collective-permute-start(bf16[1024,384]{1,0:T(8,128)(2,1)S(1)} %get-tuple-element.44), channel_id=1, source_target_pairs={{0,24},{2,26},{4,28},{6,30},{8,16},{10,18},{12,20},{14,22},{16,8},... | collective-permute-start | bytes 2359304 | tf_op jit(solution)/shard_map/ppermute | solution.py:39
  587.0 1.9 copy-start.10
  590.4 10.0 %collective-permute-start.28 = (f32[1024,512]{0,1:T(8,128)}, f32[1024,512]{0,1:T(8,128)}, u32[]{:S(2)}, u32[]{:S(2)}) collective-permute-start(f32[1024,512]{0,1:T(8,128)} %constant_dynamic-slice_fusion.4), channel_id=1, source_target_pairs={{0,1},{1,0},{2,3},{3,2},{4,5},{5,4},{6,7},{7,6},{8,9},{9,8},{10,11... | collective-permute-start | bytes 6291464 | tf_op jit(solution)/shard_map/ppermute | solution.py:51
  603.8 1.3 copy-start.11
  605.2 10.1 %collective-permute-start.29 = (bf16[256,512]{0,1:T(8,128)(2,1)S(1)}, bf16[256,512]{0,1:T(8,128)(2,1)S(1)}, u32[]{:S(2)}, u32[]{:S(2)}) collective-permute-start(bf16[256,512]{0,1:T(8,128)(2,1)S(1)} %get-tuple-element.87), channel_id=1, source_target_pairs={{0,8},{2,10},{4,12},{6,14},{8,0},{10,2},{12,4},{14,6},{16,24},{18,... | collective-permute-start | bytes 786440 | tf_op jit(solution)/shard_map/ppermute | solution.py:39
  605.2 13.1 %collective-permute-start.30 = (bf16[256,512]{0,1:T(8,128)(2,1)S(1)}, bf16[256,512]{0,1:T(8,128)(2,1)S(1)}, u32[]{:S(2)}, u32[]{:S(2)}) collective-permute-start(bf16[256,512]{0,1:T(8,128)(2,1)S(1)} %get-tuple-element.86), channel_id=1, source_target_pairs={{0,16},{2,18},{4,20},{6,22},{8,24},{10,26},{12,28},{14,30},{16,0},... | collective-permute-start | bytes 786440 | tf_op jit(solution)/shard_map/ppermute | solution.py:39
  606.6 23.9 %collective-permute-start.31 = (bf16[256,512]{0,1:T(8,128)(2,1)S(1)}, bf16[256,512]{0,1:T(8,128)(2,1)S(1)}, u32[]{:S(2)}, u32[]{:S(2)}) collective-permute-start(bf16[256,512]{0,1:T(8,128)(2,1)S(1)} %get-tuple-element.85), channel_id=1, source_target_pairs={{0,24},{2,26},{4,28},{6,30},{8,16},{10,18},{12,20},{14,22},{16,8},... | collective-permute-start | bytes 786440 | tf_op jit(solution)/shard_map/ppermute | solution.py:39
  618.3 13.3 %copy-start.16 = (bf16[256,512]{0,1:T(8,128)(2,1)}, bf16[256,512]{0,1:T(8,128)(2,1)S(1)}, u32[]{:S(2)}) copy-start(bf16[256,512]{0,1:T(8,128)(2,1)S(1)} %collective-permute-done.30) | copy-start | bytes 786436
  630.5 1.1 copy-start.17
  631.6 5.5 collective-permute-start.32
  643.8 4.7 copy-start.12
  643.8 4.7 copy-start.23
  648.5 8.7 %copy-start.20 = (s32[2048]{0:T(1024)S(1)}, s32[2048]{0:T(1024)}, u32[]{:S(2)}) copy-start(s32[2048]{0:T(1024)} %param.21) | copy-start | bytes 24580
  650.4 0.7 copy-start.15
  652.0 10.1 %collective-permute-start.33 = (bf16[23,1024]{0,1:T(8,128)(2,1)}, bf16[23,1024]{0,1:T(8,128)(2,1)}, u32[]{:S(2)}, u32[]{:S(2)}) collective-permute-start(bf16[23,1024]{0,1:T(8,128)(2,1)} %get-tuple-element.92), channel_id=1, source_target_pairs={{0,2},{2,4},{4,6},{6,8},{8,10},{10,12},{12,14},{14,16},{16,18},{18... | collective-permute-start | bytes 141320 | tf_op jit(solution)/shard_map/ppermute | solution.py:27
  653.9 14.7 %collective-permute-start.34 = (bf16[23,1024]{0,1:T(8,128)(2,1)}, bf16[23,1024]{0,1:T(8,128)(2,1)}, u32[]{:S(2)}, u32[]{:S(2)}) collective-permute-start(bf16[23,1024]{0,1:T(8,128)(2,1)} %get-tuple-element.93), channel_id=1, source_target_pairs={{2,0},{4,2},{6,4},{8,6},{10,8},{12,10},{14,12},{16,14},{18,16},{20... | collective-permute-start | bytes 141320 | tf_op jit(solution)/shard_map/ppermute | solution.py:28
  672.9 1.0 copy-start.1
  673.8 0.8 copy-start.2
  674.7 15.1 %copy-start.18 = (bf16[512,1024]{1,0:T(8,128)(2,1)S(1)}, bf16[512,1024]{1,0:T(8,128)(2,1)}, u32[]{:S(2)}) copy-start(bf16[512,1024]{1,0:T(8,128)(2,1)} %param.26) | copy-start | bytes 3145732
  688.5 5.7 collective-permute-start.35
  689.8 4.5 collective-permute-start.36
  691.2 4.4 copy-start.4
